TPU v7x, 512 devices: a whole 4x8x8 slice. The times are simulated.
512 devices in a mesh: gx: 8 (over z_hi, core), gy: 4 (over x), gz: 16 (over y, z_lo).
Axes of the slice: x: 4, y: 8, z: 8 (z_hi: 4, z_lo: 2; z = z_hi * 2 + z_lo), core: 2. Of those that a mesh axis runs over, the one named last changes fastest.
Arguments:
- segments: float32 [16, 16, 64, 9, 128], P('gx', 'gy', 'gz'), may hold values from -4 to 4, as said below
- seg_count: int32 [16, 16, 64], P('gx', 'gy', 'gz'), may hold values from 65 to 128
- pair_offsets: int32 [16, 16, 64, 13], P('gx', 'gy', 'gz'), may hold values from 8 to 26, as said below
- pair_count: int32 [16, 16, 64], P('gx', 'gy', 'gz'), may hold values from 0 to 13
- node_segs: int32 [16, 16, 64, 2, 128], P('gx', 'gy', 'gz'), may hold values from 0 to 127, as said below
Outputs:
- seg_force: float32 [16, 16, 64, 3, 128], P('gx', 'gy', 'gz')
- velocity: float32 [16, 16, 64, 3, 128], P('gx', 'gy', 'gz')
Inputs may be any that keep to these rules, and one draw needn't show every extreme that they name: `segments`: components 0 to 2 lie in [-0.5, 0.5]. `pair_offsets`: each block's 13 codes are distinct and are exactly the offsets o with o_x + o_y + o_z > 0, or with o_x + o_y + o_z == 0 and code > 13. `node_segs`: every entry of a block is below that block's seg_count.
All inputs are finite; a program needn't handle non-finite values.
Results may differ from a plain program's by a relative error of at most 0.0003.
Values sent between devices are 32-bit elements; how exact they have to be, the bound alone decides.
A program may use at most 128 MiB of HBM per device.

v0:
```python
import math

import jax
import jax.numpy as jnp
import numpy as np
from jax import lax
from jax.sharding import PartitionSpec as P

CORE = 0.3
NEAR_SCALE = 0.02
FAR_SCALE = 0.05
LENGTH = 1.5
CLIMB = 0.1


def padded_2(cells, sides, width):
    for axis, dim in sides:
        count = lax.axis_size(axis)
        head = lax.slice_in_dim(cells, 0, width, axis=dim)
        tail = lax.slice_in_dim(cells, cells.shape[dim] - width, cells.shape[dim], axis=dim)
        cells = jnp.concatenate(
            [
                lax.ppermute(tail, axis, [(i, (i + 1) % count) for i in range(count)]),
                cells,
                lax.ppermute(head, axis, [((i + 1) % count, i) for i in range(count)]),
            ],
            axis=dim,
        )
    return cells


def passed_along(block, axis, distance):
    devices = range(lax.axis_size(axis))
    route = [((i - distance) % len(devices), i) for i in devices]
    return lax.ppermute(block, axis, route)


def exponents():
    exponent_rows = []
    for degree in range(5):
        for power_x in range(degree, -1, -1):
            for power_y in range(degree - power_x, -1, -1):
                exponent_rows.append((power_x, power_y, degree - power_x - power_y))
    return np.array(exponent_rows, dtype=np.int32)


def masked_data(segments, seg_count):
    per_block = segments.shape[-1]
    living = (
        lax.broadcasted_iota(jnp.int32, seg_count.shape + (per_block,), seg_count.ndim)
        < seg_count[..., None]
    )
    keeper = living.astype(segments.dtype)[..., None, :]
    return jnp.concatenate([segments[..., :3, :], segments[..., 3:, :] * keeper], axis=-2)


def near_tile(target, source, offset_vec):
    separation = [
        source[axis_num][None, :] + offset_vec[axis_num] - target[axis_num][:, None]
        for axis_num in range(3)
    ]
    burgers_dot = sum((target[3 + comp][:, None] * source[3 + comp][None, :] for comp in range(3)))
    lines_dot = sum((target[6 + comp][:, None] * source[6 + comp][None, :] for comp in range(3)))
    cross_one = sum((target[3 + comp][:, None] * source[6 + comp][None, :] for comp in range(3)))
    cross_two = sum((target[6 + comp][:, None] * source[3 + comp][None, :] for comp in range(3)))
    coupling = burgers_dot * lines_dot - 2.0 * cross_one * cross_two
    squared = (
        separation[0] * separation[0]
        + separation[1] * separation[1]
        + separation[2] * separation[2]
        + CORE * CORE
    )
    inverse = lax.rsqrt(squared)
    inverse_cube = inverse * inverse * inverse
    weight = (
        NEAR_SCALE
        * coupling
        * (inverse_cube + 1.5 * CORE * CORE * inverse_cube * inverse * inverse)
    )
    on_target = jnp.stack([jnp.sum(weight * separation[axis_num], axis=1) for axis_num in range(3)])
    on_source = -jnp.stack(
        [jnp.sum(weight * separation[axis_num], axis=0) for axis_num in range(3)]
    )
    return (on_target, on_source)


def block_moments(masked):
    extent_x, extent_y, extent_z, channels, per_block = masked.shape
    relative = []
    for axis_num in range(3):
        parity = (
            lax.broadcasted_iota(jnp.int32, (extent_x, extent_y, extent_z), axis_num) % 2
        ).astype(masked.dtype) - 0.5
        relative.append(masked[:, :, :, axis_num, :] + parity[..., None])
    powers = [
        jnp.stack(
            [
                jnp.ones_like(value),
                value,
                value * value,
                value * value * value,
                value * value * value * value,
            ]
        )
        for value in relative
    ]
    table = exponents()
    monomial = powers[0][table[:, 0]] * powers[1][table[:, 1]] * powers[2][table[:, 2]]
    per_cell = jnp.einsum(
        "pxyzs,xyzcs->pcxyz", monomial, masked[:, :, :, 3:6, :], precision=lax.Precision.HIGHEST
    )
    count = table.shape[0]
    per_cell = per_cell.reshape(count, 3, extent_x // 2, 2, extent_y // 2, 2, extent_z // 2, 2)
    return per_cell.sum(axis=(3, 5, 7))


def kernel_derivatives(distance):
    functions = [lambda radius: 1.0 / jnp.sqrt(1.0 + (radius / LENGTH) ** 2)]
    for order_index in range(5):
        functions.append(jax.grad(functions[-1]))
    flattened = distance.reshape(-1)
    return jnp.stack(
        [jax.vmap(function)(flattened).reshape(distance.shape) for function in functions]
    )


def axis_tables(start, count, total):
    target = start + jnp.arange(count, dtype=jnp.int32)
    source = jnp.arange(total, dtype=jnp.int32)
    distance = (target[:, None] - source[None, :] + total // 2) % total - total // 2
    derivative = kernel_derivatives(2.0 * distance.astype(jnp.float32))
    factors = jnp.asarray(
        np.array([(-1.0) ** order / math.factorial(order) for order in range(5)]), derivative.dtype
    )
    value_table = derivative[:5] * factors[:, None, None]
    slope_table = derivative[1:] * factors[:, None, None]
    return (value_table, slope_table)


def far_field(moments, tables_x, tables_y, tables_z):
    table = exponents()

    def stacked(tables, axis_num):
        value_table, slope_table = tables
        chosen = [
            (
                slope_table[table[:, axis_num]]
                if direction == axis_num
                else value_table[table[:, axis_num]]
            )
            for direction in range(3)
        ]
        return jnp.stack(chosen, axis=1)

    highest = lax.Precision.HIGHEST
    first_pass = jnp.einsum("pcxyz,pdix->pdciyz", moments, stacked(tables_x, 0), precision=highest)
    second_pass = jnp.einsum(
        "pdciyz,pdjy->pdcijz", first_pass, stacked(tables_y, 1), precision=highest
    )
    return -jnp.einsum("pdcijz,pdkz->dcijk", second_pass, stacked(tables_z, 2), precision=highest)


def far_force(expansion, masked):
    spread = jnp.repeat(jnp.repeat(jnp.repeat(expansion, 2, axis=2), 2, axis=3), 2, axis=4)
    return FAR_SCALE * jnp.einsum(
        "dcxyz,xyzcs->xyzds", spread, masked[:, :, :, 3:6, :], precision=lax.Precision.HIGHEST
    )


def node_velocity(force, masked, node_segs, seg_count):
    per_block = force.shape[-1]
    shape = node_segs.shape[:-2] + (per_block, per_block)
    column = lax.broadcasted_iota(jnp.int32, shape, len(shape) - 1)
    first_pick = (node_segs[..., 0, :, None] == column).astype(force.dtype)
    second_pick = (node_segs[..., 1, :, None] == column).astype(force.dtype)
    highest = lax.Precision.HIGHEST
    node_force = 0.5 * jnp.einsum(
        "...cs,...ns->...cn", force, first_pick + second_pick, precision=highest
    )
    tangent = jnp.einsum("...cs,...ns->...cn", masked[..., 6:9, :], first_pick, precision=highest)
    burgers = jnp.einsum("...cs,...ns->...cn", masked[..., 3:6, :], first_pick, precision=highest)
    normal = jnp.stack(
        [
            tangent[..., 1, :] * burgers[..., 2, :] - tangent[..., 2, :] * burgers[..., 1, :],
            tangent[..., 2, :] * burgers[..., 0, :] - tangent[..., 0, :] * burgers[..., 2, :],
            tangent[..., 0, :] * burgers[..., 1, :] - tangent[..., 1, :] * burgers[..., 0, :],
        ],
        axis=-2,
    )
    along_normal = jnp.sum(node_force * normal, axis=-2, keepdims=True)
    norm_square = jnp.maximum(jnp.sum(normal * normal, axis=-2, keepdims=True), 1.0)
    moving = node_force - (1.0 - CLIMB) * along_normal * normal / norm_square
    living = (
        lax.broadcasted_iota(jnp.int32, seg_count.shape + (per_block,), seg_count.ndim)
        < seg_count[..., None]
    )
    return moving * living.astype(force.dtype)[..., None, :]


def local(segments, seg_count, pair_offsets, pair_count, node_segs):
    extent_x, extent_y, extent_z, channels, per_block = segments.shape
    masked = masked_data(segments, seg_count)
    padded = padded_2(masked, (("gx", 0), ("gy", 1), ("gz", 2)), 1)
    moments = block_moments(masked)
    cells_x, cells_y, cells_z = (extent_x // 2, extent_y // 2, extent_z // 2)
    devices_x, devices_y, devices_z = (
        lax.axis_size("gx"),
        lax.axis_size("gy"),
        lax.axis_size("gz"),
    )
    total_x, total_y, total_z = (cells_x * devices_x, cells_y * devices_y, cells_z * devices_z)
    monomials = moments.shape[0]
    start_x = lax.axis_index("gx") * cells_x
    start_y = lax.axis_index("gy") * cells_y
    start_z = lax.axis_index("gz") * cells_z
    placed = lax.dynamic_update_slice(
        jnp.zeros((monomials, 3, total_x, total_y, total_z), jnp.float32),
        moments,
        (jnp.int32(0), jnp.int32(0), start_x, start_y, start_z),
    )
    all_moments = lax.psum(placed, ("gx", "gy", "gz"))
    expansion = far_field(
        all_moments,
        axis_tables(start_x, cells_x, total_x),
        axis_tables(start_y, cells_y, total_y),
        axis_tables(start_z, cells_z, total_z),
    )
    pad_x, pad_y, pad_z = (extent_x + 2, extent_y + 2, extent_z + 2)
    padded_flat = padded.reshape(pad_x * pad_y * pad_z, channels, per_block)
    own_total = extent_x * extent_y * extent_z
    position = jnp.arange(own_total, dtype=jnp.int32)
    block_x = position // (extent_y * extent_z)
    block_y = position // extent_z % extent_y
    block_z = position % extent_z
    own_index = ((block_x + 1) * pad_y + block_y + 1) * pad_z + block_z + 1
    own_blocks = masked.reshape(own_total, channels, per_block)
    slot_codes = pair_offsets.reshape(own_total, -1)
    slot_counts = pair_count.reshape(own_total)
    zero_offset = jnp.zeros((3,), jnp.float32)
    selfs = jax.vmap(lambda single: near_tile(single, single, zero_offset)[0])(own_blocks)
    totals = jnp.zeros((pad_x * pad_y * pad_z, 3, per_block), jnp.float32).at[own_index].add(selfs)

    def one_slot(slot_index, totals):
        slot_code = slot_codes[:, slot_index]
        step_x = slot_code // 9 - 1
        step_y = slot_code // 3 % 3 - 1
        step_z = slot_code % 3 - 1
        neighbour = (
            ((block_x + 1 + step_x) * pad_y + block_y + 1 + step_y) * pad_z + block_z + 1 + step_z
        )
        offset_vec = jnp.stack([step_x, step_y, step_z], axis=1).astype(jnp.float32)
        on_target, on_source = jax.vmap(near_tile)(own_blocks, padded_flat[neighbour], offset_vec)
        slot_live = (slot_index < slot_counts).astype(jnp.float32)[:, None, None]
        totals = totals.at[own_index].add(on_target * slot_live)
        return totals.at[neighbour].add(on_source * slot_live)

    totals = lax.fori_loop(0, slot_codes.shape[1], one_slot, totals)
    totals = totals.reshape(pad_x, pad_y, pad_z, 3, per_block)
    for direction, source_plane, target_plane in ((-1, 0, extent_z), (1, extent_z + 1, 1)):
        returned = passed_along(totals[:, :, source_plane], "gz", direction)
        totals = totals.at[:, :, target_plane].add(returned)
    totals = totals[:, :, 1 : extent_z + 1]
    for direction, source_plane, target_plane in ((-1, 0, extent_y), (1, extent_y + 1, 1)):
        returned = passed_along(totals[:, source_plane], "gy", direction)
        totals = totals.at[:, target_plane].add(returned)
    totals = totals[:, 1 : extent_y + 1]
    for direction, source_plane, target_plane in ((-1, 0, extent_x), (1, extent_x + 1, 1)):
        returned = passed_along(totals[source_plane], "gx", direction)
        totals = totals.at[target_plane].add(returned)
    near_part = totals[1 : extent_x + 1]
    seg_force = near_part + far_force(expansion, masked)
    velocity = node_velocity(seg_force, masked, node_segs, seg_count)
    return (seg_force, velocity)


def solution(mesh):
    placed = (
        P("gx", "gy", "gz", None, None),
        P("gx", "gy", "gz"),
        P("gx", "gy", "gz", None),
        P("gx", "gy", "gz"),
        P("gx", "gy", "gz", None, None),
    )
    return jax.shard_map(
        local,
        mesh=mesh,
        in_specs=placed,
        out_specs=(P("gx", "gy", "gz", None, None), P("gx", "gy", "gz", None, None)),
        check_vma=False,
    )
```

profile of v0, /device:TPU:1, one launch (start us, length us, event | category | flops | bytes accessed | tf_op | source)
XLA Modules:
  0.0 376.2 jit_solution(18425382329735453639)
XLA Ops:
  20.3 10.7 %dynamic_update_slice.3 = f32[35,3,8,8,32]{4,2,3,1,0:T(8,128)S(1)} dynamic-update-slice(f32[35,3,8,8,32]{4,2,3,1,0:T(8,128)S(1)} %broadcast_in_dim.93, f32[35,3,1,2,2]{4,2,3,1,0:T(1,128)} %bitcast.309, s32[]{:T(128)} %copy.325, s32[]{:T(128)} %copy.325, s32[]{:T(128)S(6)} %select_n.425, s32[]{:T(128)S(6)} %select_n.426, s32[]{:T(128)S(6)} %select_n.427) | dynamic-update-slice | bytes 3364 | tf_op jit(solution)/shard_map/dynamic_update_slice | solution.py:216
  33.7 7.2 %collective-permute-start = (f32[1,4,4,9,128]{4,3,0,2,1:T(8,128)S(1)}, f32[1,4,4,9,128]{4,3,0,2,1:T(8,128)S(1)}, u32[]{:S(2)}, u32[]{:S(2)}) collective-permute-start(f32[1,4,4,9,128]{4,3,0,2,1:T(8,128)S(1)} %get-tuple-element.471), channel_id=1, source_target_pairs={{0,64},{64,128},{128,192},{192,256},{256,320},{320,384},{384,448},... | collective-permute-start | bytes 221192 | tf_op jit(solution)/shard_map/ppermute | solution.py:23
  47.8 7.6 %fusion.39 = (f32[32,128]{1,0:T(8,128)S(1)}, f32[32,128]{1,0:T(8,128)S(1)}, f32[32,128]{1,0:T(8,128)S(1)}) fusion(f32[32,128]{1,0:T(8,128)S(1)} %get-tuple-element.486, f32[32,128]{1,0:T(8,128)S(1)} %get-tuple-element.484, f32[32,128]{1,0:T(8,128)S(1)} %get-tuple-element.485, f32[32,128]{1,0:T(8,128)S(1)} %get-tuple-element.487, ...), kind=kLoop, calls=%fused_computation.105 | loop fusion | flops 24629248 | bytes 196608 | tf_op jit(solution)/shard_map/vmap()/reduce_sum | solution.py:80
  70.6 30.8 %collective-permute-start.4 = (f32[4,6,1,9,128]{4,3,0,2,1:T(8,128)S(1)}, f32[4,6,1,9,128]{4,3,0,2,1:T(8,128)S(1)}, u32[]{:S(2)}, u32[]{:S(2)}) collective-permute-start(f32[4,6,1,9,128]{4,3,0,2,1:T(8,128)S(1)} %get-tuple-element.467), channel_id=1, source_target_pairs={{0,1},{1,2},{2,3},{3,4},{4,5},{5,6},{6,7},{7,8},{8,9},{9,10},{10,1... | collective-permute-start | bytes 331784 | tf_op jit(solution)/shard_map/ppermute | solution.py:23
  110.2 161.2 %while.23 = (s32[]{:T(128)}, f32[144,3,128]{2,1,0:T(4,128)S(1)}, f32[32,9,128]{2,0,1:T(8,128)S(1)}, s32[32,13]{0,1:T(8,128)S(1)}, f32[144,9,128]{2,1,0:T(8,128)S(1)}, /*index=5*/s32[32]{0:T(128)S(1)}, s32[]{:T(128)}) while((s32[]{:T(128)}, f32[144,3,128]{2,1,0:T(4,128)S(1)}, f32[32,9,128]{2,0,1:T(8,128)S(1)}, ...), condition=%wide.region_13.14_spmd.clone, body=%wide.region_4.0_spmd.clone.sunk | while | flops 26317536 | bytes 1973845 | solution.py:257
  111.1 8.0 %fusion.270 = (f32[32,128]{1,0:T(8,128)S(1)}, f32[32,128]{1,0:T(8,128)S(1)}, f32[32,128]{1,0:T(8,128)S(1)}, f32[32,128]{1,0:T(8,128)S(1)}, f32[32,128]{1,0:T(8,128)S(1)}, /*index=5*/f32[32,128]{1,0:T(8,128)S(1)}) fusion(f32[32,128]{1,0:T(8,128)S(1)} %get-tuple-element.604, f32[32,128]{1,0:T(8,128)S(1)} %bitcast.312, ...), kind=kLoop, calls=%fused_computation.31.clone.1 | loop fusion | flops 26189824 | bytes 393216 | tf_op jit(solution)/shard_map/while/body/eval_jaxpr/vmap()/reduce_sum | solution.py:82
  123.5 8.0 %fusion.270 = (f32[32,128]{1,0:T(8,128)S(1)}, f32[32,128]{1,0:T(8,128)S(1)}, f32[32,128]{1,0:T(8,128)S(1)}, f32[32,128]{1,0:T(8,128)S(1)}, f32[32,128]{1,0:T(8,128)S(1)}, /*index=5*/f32[32,128]{1,0:T(8,128)S(1)}) fusion(f32[32,128]{1,0:T(8,128)S(1)} %get-tuple-element.604, f32[32,128]{1,0:T(8,128)S(1)} %bitcast.312, ...), kind=kLoop, calls=%fused_computation.31.clone.1 | loop fusion | flops 26189824 | bytes 393216 | tf_op jit(solution)/shard_map/while/body/eval_jaxpr/vmap()/reduce_sum | solution.py:82
  135.9 8.0 %fusion.270 = (f32[32,128]{1,0:T(8,128)S(1)}, f32[32,128]{1,0:T(8,128)S(1)}, f32[32,128]{1,0:T(8,128)S(1)}, f32[32,128]{1,0:T(8,128)S(1)}, f32[32,128]{1,0:T(8,128)S(1)}, /*index=5*/f32[32,128]{1,0:T(8,128)S(1)}) fusion(f32[32,128]{1,0:T(8,128)S(1)} %get-tuple-element.604, f32[32,128]{1,0:T(8,128)S(1)} %bitcast.312, ...), kind=kLoop, calls=%fused_computation.31.clone.1 | loop fusion | flops 26189824 | bytes 393216 | tf_op jit(solution)/shard_map/while/body/eval_jaxpr/vmap()/reduce_sum | solution.py:82
  148.3 8.0 %fusion.270 = (f32[32,128]{1,0:T(8,128)S(1)}, f32[32,128]{1,0:T(8,128)S(1)}, f32[32,128]{1,0:T(8,128)S(1)}, f32[32,128]{1,0:T(8,128)S(1)}, f32[32,128]{1,0:T(8,128)S(1)}, /*index=5*/f32[32,128]{1,0:T(8,128)S(1)}) fusion(f32[32,128]{1,0:T(8,128)S(1)} %get-tuple-element.604, f32[32,128]{1,0:T(8,128)S(1)} %bitcast.312, ...), kind=kLoop, calls=%fused_computation.31.clone.1 | loop fusion | flops 26189824 | bytes 393216 | tf_op jit(solution)/shard_map/while/body/eval_jaxpr/vmap()/reduce_sum | solution.py:82
  160.7 8.0 %fusion.270 = (f32[32,128]{1,0:T(8,128)S(1)}, f32[32,128]{1,0:T(8,128)S(1)}, f32[32,128]{1,0:T(8,128)S(1)}, f32[32,128]{1,0:T(8,128)S(1)}, f32[32,128]{1,0:T(8,128)S(1)}, /*index=5*/f32[32,128]{1,0:T(8,128)S(1)}) fusion(f32[32,128]{1,0:T(8,128)S(1)} %get-tuple-element.604, f32[32,128]{1,0:T(8,128)S(1)} %bitcast.312, ...), kind=kLoop, calls=%fused_computation.31.clone.1 | loop fusion | flops 26189824 | bytes 393216 | tf_op jit(solution)/shard_map/while/body/eval_jaxpr/vmap()/reduce_sum | solution.py:82
  173.1 8.0 %fusion.270 = (f32[32,128]{1,0:T(8,128)S(1)}, f32[32,128]{1,0:T(8,128)S(1)}, f32[32,128]{1,0:T(8,128)S(1)}, f32[32,128]{1,0:T(8,128)S(1)}, f32[32,128]{1,0:T(8,128)S(1)}, /*index=5*/f32[32,128]{1,0:T(8,128)S(1)}) fusion(f32[32,128]{1,0:T(8,128)S(1)} %get-tuple-element.604, f32[32,128]{1,0:T(8,128)S(1)} %bitcast.312, ...), kind=kLoop, calls=%fused_computation.31.clone.1 | loop fusion | flops 26189824 | bytes 393216 | tf_op jit(solution)/shard_map/while/body/eval_jaxpr/vmap()/reduce_sum | solution.py:82
  185.5 8.0 %fusion.270 = (f32[32,128]{1,0:T(8,128)S(1)}, f32[32,128]{1,0:T(8,128)S(1)}, f32[32,128]{1,0:T(8,128)S(1)}, f32[32,128]{1,0:T(8,128)S(1)}, f32[32,128]{1,0:T(8,128)S(1)}, /*index=5*/f32[32,128]{1,0:T(8,128)S(1)}) fusion(f32[32,128]{1,0:T(8,128)S(1)} %get-tuple-element.604, f32[32,128]{1,0:T(8,128)S(1)} %bitcast.312, ...), kind=kLoop, calls=%fused_computation.31.clone.1 | loop fusion | flops 26189824 | bytes 393216 | tf_op jit(solution)/shard_map/while/body/eval_jaxpr/vmap()/reduce_sum | solution.py:82
  197.9 8.0 %fusion.270 = (f32[32,128]{1,0:T(8,128)S(1)}, f32[32,128]{1,0:T(8,128)S(1)}, f32[32,128]{1,0:T(8,128)S(1)}, f32[32,128]{1,0:T(8,128)S(1)}, f32[32,128]{1,0:T(8,128)S(1)}, /*index=5*/f32[32,128]{1,0:T(8,128)S(1)}) fusion(f32[32,128]{1,0:T(8,128)S(1)} %get-tuple-element.604, f32[32,128]{1,0:T(8,128)S(1)} %bitcast.312, ...), kind=kLoop, calls=%fused_computation.31.clone.1 | loop fusion | flops 26189824 | bytes 393216 | tf_op jit(solution)/shard_map/while/body/eval_jaxpr/vmap()/reduce_sum | solution.py:82
  210.3 8.0 %fusion.270 = (f32[32,128]{1,0:T(8,128)S(1)}, f32[32,128]{1,0:T(8,128)S(1)}, f32[32,128]{1,0:T(8,128)S(1)}, f32[32,128]{1,0:T(8,128)S(1)}, f32[32,128]{1,0:T(8,128)S(1)}, /*index=5*/f32[32,128]{1,0:T(8,128)S(1)}) fusion(f32[32,128]{1,0:T(8,128)S(1)} %get-tuple-element.604, f32[32,128]{1,0:T(8,128)S(1)} %bitcast.312, ...), kind=kLoop, calls=%fused_computation.31.clone.1 | loop fusion | flops 26189824 | bytes 393216 | tf_op jit(solution)/shard_map/while/body/eval_jaxpr/vmap()/reduce_sum | solution.py:82
  222.7 8.0 %fusion.270 = (f32[32,128]{1,0:T(8,128)S(1)}, f32[32,128]{1,0:T(8,128)S(1)}, f32[32,128]{1,0:T(8,128)S(1)}, f32[32,128]{1,0:T(8,128)S(1)}, f32[32,128]{1,0:T(8,128)S(1)}, /*index=5*/f32[32,128]{1,0:T(8,128)S(1)}) fusion(f32[32,128]{1,0:T(8,128)S(1)} %get-tuple-element.604, f32[32,128]{1,0:T(8,128)S(1)} %bitcast.312, ...), kind=kLoop, calls=%fused_computation.31.clone.1 | loop fusion | flops 26189824 | bytes 393216 | tf_op jit(solution)/shard_map/while/body/eval_jaxpr/vmap()/reduce_sum | solution.py:82
  235.1 8.0 %fusion.270 = (f32[32,128]{1,0:T(8,128)S(1)}, f32[32,128]{1,0:T(8,128)S(1)}, f32[32,128]{1,0:T(8,128)S(1)}, f32[32,128]{1,0:T(8,128)S(1)}, f32[32,128]{1,0:T(8,128)S(1)}, /*index=5*/f32[32,128]{1,0:T(8,128)S(1)}) fusion(f32[32,128]{1,0:T(8,128)S(1)} %get-tuple-element.604, f32[32,128]{1,0:T(8,128)S(1)} %bitcast.312, ...), kind=kLoop, calls=%fused_computation.31.clone.1 | loop fusion | flops 26189824 | bytes 393216 | tf_op jit(solution)/shard_map/while/body/eval_jaxpr/vmap()/reduce_sum | solution.py:82
  247.5 8.0 %fusion.270 = (f32[32,128]{1,0:T(8,128)S(1)}, f32[32,128]{1,0:T(8,128)S(1)}, f32[32,128]{1,0:T(8,128)S(1)}, f32[32,128]{1,0:T(8,128)S(1)}, f32[32,128]{1,0:T(8,128)S(1)}, /*index=5*/f32[32,128]{1,0:T(8,128)S(1)}) fusion(f32[32,128]{1,0:T(8,128)S(1)} %get-tuple-element.604, f32[32,128]{1,0:T(8,128)S(1)} %bitcast.312, ...), kind=kLoop, calls=%fused_computation.31.clone.1 | loop fusion | flops 26189824 | bytes 393216 | tf_op jit(solution)/shard_map/while/body/eval_jaxpr/vmap()/reduce_sum | solution.py:82
  259.9 8.0 %fusion.270 = (f32[32,128]{1,0:T(8,128)S(1)}, f32[32,128]{1,0:T(8,128)S(1)}, f32[32,128]{1,0:T(8,128)S(1)}, f32[32,128]{1,0:T(8,128)S(1)}, f32[32,128]{1,0:T(8,128)S(1)}, /*index=5*/f32[32,128]{1,0:T(8,128)S(1)}) fusion(f32[32,128]{1,0:T(8,128)S(1)} %get-tuple-element.604, f32[32,128]{1,0:T(8,128)S(1)} %bitcast.312, ...), kind=kLoop, calls=%fused_computation.31.clone.1 | loop fusion | flops 26189824 | bytes 393216 | tf_op jit(solution)/shard_map/while/body/eval_jaxpr/vmap()/reduce_sum | solution.py:82
  271.4 5.4 %collective-permute-start.6 = (f32[4,6,3,128]{3,2,0,1:T(4,128)S(1)}, f32[4,6,3,128]{3,2,0,1:T(4,128)S(1)}, u32[]{:S(2)}, u32[]{:S(2)}) collective-permute-start(f32[4,6,3,128]{3,2,0,1:T(4,128)S(1)} %slice_bitcast_fusion.14), channel_id=1, source_target_pairs={{1,0},{2,1},{3,2},{4,3},{5,4},{6,5},{7,6},{8,7},{9,8},{10,9},{11,1... | collective-permute-start | bytes 110600 | tf_op jit(solution)/shard_map/ppermute | solution.py:35
  279.9 5.3 %collective-permute-done.7 = f32[4,6,3,128]{3,2,0,1:T(4,128)S(1)} collective-permute-done((f32[4,6,3,128]{3,2,0,1:T(4,128)S(1)}, f32[4,6,3,128]{3,2,0,1:T(4,128)S(1)}, u32[]{:S(2)}, u32[]{:S(2)}) %collective-permute-start.7) | collective-permute-done | bytes 36896 | tf_op jit(solution)/shard_map/ppermute | solution.py:35
  296.8 12.2 %collective-permute-start.10 = (f32[4,4,3,128]{3,2,1,0:T(4,128)S(1)}, f32[4,4,3,128]{3,2,1,0:T(4,128)S(1)}, u32[]{:S(2)}, u32[]{:S(2)}) collective-permute-start(f32[4,4,3,128]{3,2,1,0:T(4,128)S(1)} %slice_bitcast_fusion.16), channel_id=1, source_target_pairs={{64,0},{128,64},{192,128},{256,192},{320,256},{384,320},{448,384},... | collective-permute-start | bytes 73736 | tf_op jit(solution)/shard_map/ppermute | solution.py:35
  318.5 32.4 %all-reduce.2.cloned.1.call-done = f32[35,3,8,8,32]{4,2,3,1,0:T(8,128)} async-done(((f32[35,3,8,8,32]{4,2,3,1,0:T(8,128)}), f32[35,3,8,8,32]{4,2,3,1,0:T(8,128)}) %all-reduce.2.cloned.1.call-update) | async-done | bytes 860176 | tf_op jit(solution)/shard_map/psum | solution.py:221
  350.9 4.9 %fusion.75 = f32[35,3,3,8,32]{4,1,3,2,0:T(4,128)S(1)} fusion(f32[35,3,8,8,32]{4,2,3,1,0:T(8,128)} %all-reduce.2.cloned.1.call-done, f32[35,1,1,8]{3,1,0,2:T(1,128)S(1)} %copy.211, f32[35,1,1,8]{3,1,0,2:T(1,128)S(1)} %copy.210), kind=kOutput, calls=%fused_computation.207 | convolution fusion | flops 7743120 | bytes 1184960 | tf_op jit(solution)/shard_map/pcxyz,pdix->pdciyz/dot_general | solution.py:156
  357.6 5.3 %fusion.58 = f32[3,3,2,2]{1,3,2,0:T(2,128)S(1)} fusion(f32[35,3,3,2,32]{0,2,4,3,1:T(4,128)S(1)} %copy.220, f32[35,1,2,32]{0,2,3,1:T(2,128)S(1)} %bitcast.332, f32[35,1,2,32]{0,2,3,1:T(2,128)S(1)} %bitcast.331), kind=kOutput, calls=%fused_computation.125 | convolution fusion | flops 497316 | bytes 98704 | tf_op jit(solution)/shard_map/pdcijz,pdkz->dcijk/dot_general | solution.py:160
  (344 shorter events, 134.3 us)
Async XLA Ops:
  7.2 343.8 %all-reduce.2.cloned.1.call-start = ((), (), s32[]{:S(2)}) async-start(), calls=%async_computation | async-start | bytes 6881280 | tf_op jit(solution)/shard_map/psum | solution.py:221
  7.3 10.1 %slice-start = ((f32[2,4,4,9,128]{4,2,3,1,0:T(4,128)}), f32[2,4,4,6,128]{4,2,3,1,0:T(4,128)S(1)}, s32[]{:S(2)}) async-start(f32[2,4,4,9,128]{4,2,3,1,0:T(4,128)} %param.46), calls=%async_computation.1 | async-start | bytes 196608 | tf_op jit(solution)/shard_map/slice | solution.py:54
  9.6 8.0 %copy-start.5 = (s32[1024]{0:T(1024)}, s32[1024]{0:T(1024)S(1)}, u32[]{:S(2)}) copy-start(s32[1024]{0:T(1024)S(1)} %pad_clamp_fusion.3) | copy-start | bytes 12292
  14.7 0.9 copy-start.6
  14.7 1.8 copy-start.7
  20.3 12.5 %slice-start.1 = ((f32[2,4,4,9,128]{4,2,3,1,0:T(4,128)}), f32[2,4,4,3,128]{4,2,3,1,0:T(4,128)S(1)}, s32[]{:S(2)}) async-start(f32[2,4,4,9,128]{4,2,3,1,0:T(4,128)} %param.46), calls=%async_computation.2 | async-start | bytes 98304 | tf_op jit(solution)/shard_map/slice | solution.py:54
  31.0 1.8 copy-start
  32.7 22.8 %copy-start.4 = (s32[2,4,4,13]{3,2,1,0:T(4,128)S(1)}, s32[2,4,4,13]{3,2,1,0:T(4,128)}, u32[]{:S(2)}) copy-start(s32[2,4,4,13]{3,2,1,0:T(4,128)} %param.48) | copy-start | bytes 4996
  32.7 22.9 %copy-start.9 = (s32[2,4,4]{2,1,0:T(4,128)S(1)}, s32[2,4,4]{2,1,0:T(4,128)}, u32[]{:S(2)}) copy-start(s32[2,4,4]{2,1,0:T(4,128)} %param.49) | copy-start | bytes 388
  32.8 22.9 %copy-start.3 = (s32[2,4,4,2,128]{4,3,2,1,0:T(2,128)S(1)}, s32[2,4,4,2,128]{4,3,2,1,0:T(2,128)}, u32[]{:S(2)}) copy-start(s32[2,4,4,2,128]{4,3,2,1,0:T(2,128)} %param.50) | copy-start | bytes 98308
  33.7 28.3 %collective-permute-start = (f32[1,4,4,9,128]{4,3,0,2,1:T(8,128)S(1)}, f32[1,4,4,9,128]{4,3,0,2,1:T(8,128)S(1)}, u32[]{:S(2)}, u32[]{:S(2)}) collective-permute-start(f32[1,4,4,9,128]{4,3,0,2,1:T(8,128)S(1)} %get-tuple-element.471), channel_id=1, source_target_pairs={{0,64},{64,128},{128,192},{192,256},{256,320},{320,384},{384,448},... | collective-permute-start | bytes 221192 | tf_op jit(solution)/shard_map/ppermute | solution.py:23
  40.9 21.1 %collective-permute-start.1 = (f32[1,4,4,9,128]{4,3,0,2,1:T(8,128)S(1)}, f32[1,4,4,9,128]{4,3,0,2,1:T(8,128)S(1)}, u32[]{:S(2)}, u32[]{:S(2)}) collective-permute-start(f32[1,4,4,9,128]{4,3,0,2,1:T(8,128)S(1)} %get-tuple-element.472), channel_id=1, source_target_pairs={{64,0},{128,64},{192,128},{256,192},{320,256},{384,320},{448,384},... | collective-permute-start | bytes 221192 | tf_op jit(solution)/shard_map/ppermute | solution.py:25
  44.5 15.6 %copy-start.8 = (f32[5]{0:T(128)S(1)}, f32[5]{0:T(128)}, u32[]{:S(2)}) copy-start(f32[5]{0:T(128)} %constant.632.clone) | copy-start | bytes 64
  46.5 15.5 %copy-start.2 = (f32[2,4,4,6,128]{4,3,0,2,1:T(8,128)S(1)}, f32[2,4,4,6,128]{4,3,0,2,1:T(8,128)}, u32[]{:S(2)}) copy-start(f32[2,4,4,6,128]{4,3,0,2,1:T(8,128)} %copy-done.1) | copy-start | bytes 294916
  62.1 6.9 %collective-permute-start.2 = (f32[4,1,4,9,128]{4,3,0,2,1:T(8,128)S(1)}, f32[4,1,4,9,128]{4,3,0,2,1:T(8,128)S(1)}, u32[]{:S(2)}, u32[]{:S(2)}) collective-permute-start(f32[4,1,4,9,128]{4,3,0,2,1:T(8,128)S(1)} %get-tuple-element.469), channel_id=1, source_target_pairs={{0,16},{16,32},{32,48},{48,0},{1,17},{17,33},{33,49},{49,1},{2,18}... | collective-permute-start | bytes 221192 | tf_op jit(solution)/shard_map/ppermute | solution.py:23
  64.0 6.5 %collective-permute-start.3 = (f32[4,1,4,9,128]{4,3,0,2,1:T(8,128)S(1)}, f32[4,1,4,9,128]{4,3,0,2,1:T(8,128)S(1)}, u32[]{:S(2)}, u32[]{:S(2)}) collective-permute-start(f32[4,1,4,9,128]{4,3,0,2,1:T(8,128)S(1)} %get-tuple-element.470), channel_id=1, source_target_pairs={{16,0},{32,16},{48,32},{0,48},{17,1},{33,17},{49,33},{1,49},{18,2}... | collective-permute-start | bytes 221192 | tf_op jit(solution)/shard_map/ppermute | solution.py:25
  70.6 37.3 %collective-permute-start.4 = (f32[4,6,1,9,128]{4,3,0,2,1:T(8,128)S(1)}, f32[4,6,1,9,128]{4,3,0,2,1:T(8,128)S(1)}, u32[]{:S(2)}, u32[]{:S(2)}) collective-permute-start(f32[4,6,1,9,128]{4,3,0,2,1:T(8,128)S(1)} %get-tuple-element.467), channel_id=1, source_target_pairs={{0,1},{1,2},{2,3},{3,4},{4,5},{5,6},{6,7},{7,8},{8,9},{9,10},{10,1... | collective-permute-start | bytes 331784 | tf_op jit(solution)/shard_map/ppermute | solution.py:23
  101.4 8.5 %collective-permute-start.5 = (f32[4,6,1,9,128]{4,3,0,2,1:T(8,128)S(1)}, f32[4,6,1,9,128]{4,3,0,2,1:T(8,128)S(1)}, u32[]{:S(2)}, u32[]{:S(2)}) collective-permute-start(f32[4,6,1,9,128]{4,3,0,2,1:T(8,128)S(1)} %get-tuple-element.468), channel_id=1, source_target_pairs={{1,0},{2,1},{3,2},{4,3},{5,4},{6,5},{7,6},{8,7},{9,8},{10,9},{11,1... | collective-permute-start | bytes 331784 | tf_op jit(solution)/shard_map/ppermute | solution.py:25
  271.4 6.4 %collective-permute-start.6 = (f32[4,6,3,128]{3,2,0,1:T(4,128)S(1)}, f32[4,6,3,128]{3,2,0,1:T(4,128)S(1)}, u32[]{:S(2)}, u32[]{:S(2)}) collective-permute-start(f32[4,6,3,128]{3,2,0,1:T(4,128)S(1)} %slice_bitcast_fusion.14), channel_id=1, source_target_pairs={{1,0},{2,1},{3,2},{4,3},{5,4},{6,5},{7,6},{8,7},{9,8},{10,9},{11,1... | collective-permute-start | bytes 110600 | tf_op jit(solution)/shard_map/ppermute | solution.py:35
  277.9 7.3 %collective-permute-start.7 = (f32[4,6,3,128]{3,2,0,1:T(4,128)S(1)}, f32[4,6,3,128]{3,2,0,1:T(4,128)S(1)}, u32[]{:S(2)}, u32[]{:S(2)}) collective-permute-start(f32[4,6,3,128]{3,2,0,1:T(4,128)S(1)} %slice_bitcast_fusion.12), channel_id=1, source_target_pairs={{15,0},{0,1},{1,2},{2,3},{3,4},{4,5},{5,6},{6,7},{7,8},{8,9},{9,10... | collective-permute-start | bytes 110600 | tf_op jit(solution)/shard_map/ppermute | solution.py:35
  285.2 5.3 %collective-permute-start.8 = (f32[4,4,3,128]{3,2,1,0:T(4,128)S(1)}, f32[4,4,3,128]{3,2,1,0:T(4,128)S(1)}, u32[]{:S(2)}, u32[]{:S(2)}) collective-permute-start(f32[4,4,3,128]{3,2,1,0:T(4,128)S(1)} %slice_bitcast_fusion.19), channel_id=1, source_target_pairs={{16,0},{32,16},{48,32},{0,48},{17,1},{33,17},{49,33},{1,49},{18,2}... | collective-permute-start | bytes 73736 | tf_op jit(solution)/shard_map/ppermute | solution.py:35
  290.6 6.2 %collective-permute-start.9 = (f32[4,4,3,128]{3,2,1,0:T(4,128)S(1)}, f32[4,4,3,128]{3,2,1,0:T(4,128)S(1)}, u32[]{:S(2)}, u32[]{:S(2)}) collective-permute-start(f32[4,4,3,128]{3,2,1,0:T(4,128)S(1)} %slice_bitcast_fusion.17), channel_id=1, source_target_pairs={{48,0},{0,16},{16,32},{32,48},{49,1},{1,17},{17,33},{33,49},{50,2}... | collective-permute-start | bytes 73736 | tf_op jit(solution)/shard_map/ppermute | solution.py:35
  296.8 17.1 %collective-permute-start.10 = (f32[4,4,3,128]{3,2,1,0:T(4,128)S(1)}, f32[4,4,3,128]{3,2,1,0:T(4,128)S(1)}, u32[]{:S(2)}, u32[]{:S(2)}) collective-permute-start(f32[4,4,3,128]{3,2,1,0:T(4,128)S(1)} %slice_bitcast_fusion.16), channel_id=1, source_target_pairs={{64,0},{128,64},{192,128},{256,192},{320,256},{384,320},{448,384},... | collective-permute-start | bytes 73736 | tf_op jit(solution)/shard_map/ppermute | solution.py:35
  313.9 49.1 %collective-permute-start.11 = (f32[4,4,3,128]{3,2,1,0:T(4,128)S(1)}, f32[4,4,3,128]{3,2,1,0:T(4,128)S(1)}, u32[]{:S(2)}, u32[]{:S(2)}) collective-permute-start(f32[4,4,3,128]{3,2,1,0:T(4,128)S(1)} %slice_bitcast_fusion.15), channel_id=1, source_target_pairs={{448,0},{0,64},{64,128},{128,192},{192,256},{256,320},{320,384},{3... | collective-permute-start | bytes 73736 | tf_op jit(solution)/shard_map/ppermute | solution.py:35
  (1 other events, 0.7 us)
Sparse Core Ops, SparseCore 0:
  32.9 318.0 all-reduce.1
where the time goes:
time: 378 us; the launch traced here: 376 us
  other arithmetic  172 us (46%)
  starting transfers between devices  83.8 us (22%)
  waiting for transfers between devices  48.6 us (13%)
  local copies, waits for them, and re-layouts  34.5 us (9%)
  matrix products  21.6 us (6%)
  between operations  14.8 us (4%)
    reduce_sum x13, other arithmetic, near_tile(): jnp.sum(weight * separation[axis_num], axis=0)  104 us
    ppermute x3, starting transfers between devices, padded_2(): lax.ppermute(tail, axis, [(i, (i + 1) % count) for i in range(count)])  39.9 us
    psum x1, waiting for transfers between devices, local(): all_moments = lax.psum(placed, ('gx', 'gy', 'gz'))  32.4 us
    ppermute x6, starting transfers between devices, passed_along(): return lax.ppermute(block, axis, route)  31 us
    scatter-add x13, other arithmetic, one_slot(): return totals.at[neighbour].add(on_source * slot_live)  21.4 us
    scatter-add x13, other arithmetic, one_slot(): totals = totals.at[own_index].add(on_target * slot_live)  21.3 us
    ppermute x3, starting transfers between devices, padded_2(): lax.ppermute(head, axis, [((i + 1) % count, i) for i in range(count)])  12.8 us
    dynamic_update_slice x1, local copies, waits for them, and re-layouts, local(): lax.dynamic_update_slice(jnp.zeros((monomials, 3, total_x, total_y, total...  10.7 us
  transfers between devices with their start and end apart: 13, of which 9 were waited for; matrix products, arithmetic and copies ran while one was open for 52% of the time, Pallas kernels for 0%

commit v1 on v0

v1 whole, which is shorter than its diff:
```python
import functools
import math

import jax
import jax.numpy as jnp
import numpy as np
from jax import lax
from jax.experimental import pallas as pl
from jax.experimental.pallas import tpu as pltpu
from jax.sharding import PartitionSpec as P

CORE = 0.3
NEAR_SCALE = 0.02
FAR_SCALE = 0.05
LENGTH = 1.5
CLIMB = 0.1

MESH = pl.DeviceIdType.MESH
F32 = jnp.float32
BF16 = jnp.bfloat16

BX, BY, BZ, SEG = 2, 4, 4, 128
PX, PY = BX + 2, BY + 2
COMPS = 10
PAIRS = 13
CHUNK = 32
LIST_ROWS = 7

GHOST_COLUMNS = (
    [(0, py) for py in range(PY)]
    + [(PX - 1, py) for py in range(PY)]
    + [(px, py) for px in (1, 2) for py in (0, PY - 1)]
)
Y_PAIRS = ((0, 5), (1, 2), (3, 4))
Z_OWN = PX * PY * BZ
Z_GHOST = Z_OWN + 2 * BX * BY
BLOCKS = Z_GHOST + 2 * len(GHOST_COLUMNS)


def block_index(px, py, pz):
    if 1 <= pz <= BZ:
        pair = next(i for i, p in enumerate(Y_PAIRS) if py in p)
        return (px * 3 + pair) * 8 + Y_PAIRS[pair].index(py) * BZ + pz - 1
    side = 0 if pz == 0 else 1
    if 1 <= px <= BX and 1 <= py <= BY:
        return Z_OWN + side * 8 + (px - 1) * BY + py - 1
    return Z_GHOST + side * 16 + GHOST_COLUMNS.index((px, py))


def step_of(code):
    return code // 9 - 1, code // 3 % 3 - 1, code % 3 - 1


def half_shell(code):
    total = sum(step_of(code))
    return total > 0 or (total == 0 and code > 13)


def neighbour_table():
    table = np.zeros((BX * BY * BZ, 128), np.float32)
    for x in range(BX):
        for y in range(BY):
            for z in range(BZ):
                for code in range(27):
                    ox, oy, oz = step_of(code)
                    table[(x * BY + y) * BZ + z, code] = block_index(x + 1 + ox, y + 1 + oy, z + 1 + oz)
    return table


def exponents():
    rows = []
    for degree in range(5):
        for power_x in range(degree, -1, -1):
            for power_y in range(degree - power_x, -1, -1):
                rows.append((power_x, power_y, degree - power_x - power_y))
    return rows


def axis_values(total):
    units = np.arange(total)
    radius = 2.0 * (((units + total // 2) % total) - total // 2).astype(np.float64)
    scale = 1.0 / LENGTH**2
    base = 1.0 + scale * radius**2
    poly = np.polynomial.Polynomial([1.0])
    derivatives = []
    for order in range(6):
        derivatives.append(poly(radius) * base ** (-(2 * order + 1) / 2))
        poly = poly.deriv() * np.polynomial.Polynomial([1.0, 0.0, scale]) - np.polynomial.Polynomial(
            [0.0, (2 * order + 1) * scale]
        ) * poly
    factor = [(-1.0) ** n / math.factorial(n) for n in range(5)]
    g = np.stack([factor[n] * derivatives[n] for n in range(5)])
    h = np.stack([factor[n] * derivatives[n + 1] for n in range(5)])
    return g, h


def far_tables(nx, ny, nz):
    powers = exponents()
    table_x = np.zeros((2, nx, 128))
    values = axis_values(nx)
    for kind in range(2):
        for r in range(nx):
            for c in range(3):
                for p, power in enumerate(powers):
                    table_x[kind, r, c * 35 + p] = values[kind][power[0], r % nx]
    table_y = np.zeros((2, 2, ny, 8, 128))
    total = 2 * ny
    values = axis_values(total)
    for kind in range(2):
        for j in range(2):
            for r in range(ny):
                for row in range(8):
                    unit = (2 * r + j - row // 4) % total
                    for c in range(3):
                        for p, power in enumerate(powers):
                            table_y[kind, j, r, row, c * 35 + p] = values[kind][power[1], unit]
    table_z = np.zeros((2, nz, 8, 128))
    total = 2 * nz
    values = axis_values(total)
    for k in range(2):
        for r in range(nz):
            for row in range(8):
                unit = (2 * r + k - row // 2 % 2) % total
                x_kind = 1 - row % 2
                for y_kind in range(2):
                    z_kind = 1 if (x_kind == 0 and y_kind == 0) else 0
                    for c in range(3):
                        for n in range(5):
                            lane = y_kind * 16 + c * 5 + n
                            table_z[k, r, row, lane] = -FAR_SCALE * values[z_kind][n, unit]
    fold = np.zeros((3, 128, 128))
    for c in range(3):
        for p, power in enumerate(powers):
            for kind in range(2):
                fold[kind, c * 35 + p, kind * 16 + c * 5 + power[2]] = 1.0
        for n in range(5):
            for kind in range(2):
                fold[2, kind * 16 + c * 5 + n, kind * 3 + c] = 1.0
    return [a.astype(np.float32) for a in (table_x, table_y, table_z, fold)]


def iota(shape, dim):
    return lax.broadcasted_iota(jnp.int32, shape, dim)


def parts(value, count):
    found = []
    for _ in range(count):
        part = value.astype(BF16).astype(F32)
        found.append(part)
        value = value - part
    return found


def exact_dot(value, zero_one):
    return sum(jnp.dot(p.astype(BF16), zero_one, preferred_element_type=F32) for p in parts(value, 3))


def exchange_kernel(
    sizes,
    seg_ref, count_ref, offset_ref, pair_count_ref, table_x, table_y, table_z, fold_ref, neighbour_ref,
    pad, z_own, z_ghost, list_ref, far_ref,
    own_face, ghost_face, got_x, got_y, got_z, code_rows,
    face_send, face_recv, z_send, z_recv, x_send, x_recv, y_send, y_recv, far_send, far_recv,
):
    nx, ny, nz = sizes
    gx, gy, gz = lax.axis_index("gx"), lax.axis_index("gy"), lax.axis_index("gz")

    def at(dx, dy, dz):
        return (lax.rem(gx + dx + nx, nx), lax.rem(gy + dy + ny, ny), lax.rem(gz + dz + nz, nz))

    peers = [(r, 0, 0) for r in range(1, nx)] + [(0, r, 0) for r in range(1, ny)] + [(0, 0, r) for r in range(1, nz)]
    peers += [(dx, dy, 0) for dx in (-1, 1) for dy in (-1, 1)]
    barrier = pltpu.get_barrier_semaphore()
    for peer in peers:
        pl.semaphore_signal(barrier, inc=1, device_id=at(*peer), device_id_type=MESH)

    def send(src, dst, send_sem, recv_sem, peer):
        copy = pltpu.make_async_remote_copy(
            src_ref=src, dst_ref=dst, send_sem=send_sem, recv_sem=recv_sem, device_id=at(*peer), device_id_type=MESH
        )
        copy.start()
        return copy

    lane = iota((BZ, SEG), 1)
    row = iota((BZ, SEG), 0)

    def column(ref, x, y):
        return jnp.sum(jnp.where(lane[:, :BZ] == row[:, :BZ], ref[x, y : y + 1, :], 0), axis=1, keepdims=True)

    for x in range(BX):
        for y in range(BY):
            count = column(count_ref, x, y)
            live = lane < count
            for c in range(9):
                value = seg_ref[x, y, c]
                pad[x + 1, y + 1, c] = value if c < 3 else jnp.where(live, value, 0.0)
            listed = column(pair_count_ref, x, y)
            offsets = offset_ref[x, y]
            codes = jnp.where(lane == 127, count, 0)
            for i in range(PAIRS):
                code = offsets[:, i : i + 1]
                code = jnp.where(i < listed, code, -64)
                codes = jnp.where((lane == code) | (lane == 90 - code), 1, codes)
            pad[x + 1, y + 1, 9] = codes.astype(F32)
    for side, z in ((0, 0), (1, BZ - 1)):
        for c in range(COMPS):
            for x in range(BX):
                for y in range(BY):
                    own_face[side, c, x * BY + y : x * BY + y + 1, :] = pad[x + 1, y + 1, c, z : z + 1, :]

    pl.semaphore_wait(barrier, len(peers))

    faces = []
    moves = [(1, 0, pad.at[2, 1:5], pad.at[0, 1:5]), (-1, 0, pad.at[1, 1:5], pad.at[3, 1:5]),
             (0, 1, pad.at[1:3, 4], pad.at[1:3, 0]), (0, -1, pad.at[1:3, 1], pad.at[1:3, 5])]
    for dx in (-1, 1):
        for dy in (-1, 1):
            moves.append((dx, dy, pad.at[2 if dx > 0 else 1, 4 if dy > 0 else 1], pad.at[0 if dx > 0 else 3, 0 if dy > 0 else 5]))
    for i, (dx, dy, src, dst) in enumerate(moves):
        faces.append(send(src, dst, face_send.at[i], face_recv.at[i], (dx, dy, 0)))
    z_faces = [
        send(own_face.at[0], z_own.at[1], z_send.at[0], z_recv.at[0], (0, 0, -1)),
        send(own_face.at[1], z_own.at[0], z_send.at[1], z_recv.at[1], (0, 0, 1)),
    ]

    row8, lane8 = iota((8, SEG), 0), iota((8, SEG), 1)
    z_part = (row8 % 2).astype(F32) - 0.5
    powers = exponents()
    totals = None
    for x in range(BX):
        for parity in range(2):
            value = [
                jnp.concatenate([pad[x + 1, parity + 1, c], pad[x + 1, parity + 3, c]], axis=0) for c in range(6)
            ]
            at_x, at_y, at_z = value[0] + (x - 0.5), value[1] + (parity - 0.5), value[2] + z_part
            mono = {}
            for power in powers:
                if sum(power) == 0:
                    continue
                axis = next(a for a in range(3) if power[a])
                lower = tuple(n - (a == axis) for a, n in enumerate(power))
                factor = (at_x, at_y, at_z)[axis]
                mono[power] = factor if sum(lower) == 0 else mono[lower] * factor
            terms = [
                value[3 + c] if sum(power) == 0 else mono[power] * value[3 + c] for c in range(3) for power in powers
            ]
            totals = terms if totals is None else [a + b for a, b in zip(totals, terms)]
    moments = jnp.zeros((8, SEG), F32)
    for i, term in enumerate(totals):
        moments = jnp.where(lane8 == i, jnp.sum(term, axis=1, keepdims=True), moments)

    got_x[0] = moments
    sent_x = [send(got_x.at[0], got_x.at[r], x_send.at[r], x_recv.at[r], (r, 0, 0)) for r in range(1, nx)]
    for copy in sent_x:
        copy.wait_recv()
    by_x = []
    for kind in range(2):
        by_x.append(sum(table_x[kind, r : r + 1, :] * got_x[r] for r in range(nx)))
    g_x, h_x = by_x
    got_y[0] = jnp.where(row8 % 2 == 0, h_x + pltpu.roll(h_x, 7, 0), g_x + pltpu.roll(g_x, 1, 0))
    sent_y = [send(got_y.at[0], got_y.at[r], y_send.at[r], y_recv.at[r], (0, r, 0)) for r in range(1, ny)]

    for copy in faces:
        copy.wait_recv()
    for side, z in ((0, 0), (1, BZ - 1)):
        for c in range(COMPS):
            for n, (px, py) in enumerate(GHOST_COLUMNS):
                ghost_face[side, c, n : n + 1, :] = pad[px, py, c, z : z + 1, :]
    z_faces += [
        send(ghost_face.at[0], z_ghost.at[1], z_send.at[2], z_recv.at[2], (0, 0, -1)),
        send(ghost_face.at[1], z_ghost.at[0], z_send.at[3], z_recv.at[3], (0, 0, 1)),
    ]

    for copy in sent_y:
        copy.wait_recv()
    by_y = []
    for kind in range(2):
        pair = []
        for j in range(2):
            value = sum(table_y[kind, j, r] * got_y[r] for r in range(ny))
            pair.append(value + pltpu.roll(value, 4, 0))
        by_y.append(jnp.where(row8 < 4, pair[0], pair[1]))
    got_z[0] = exact_dot(by_y[0], fold_ref[0]) + exact_dot(by_y[1], fold_ref[1])
    sent_z = [send(got_z.at[0], got_z.at[r], far_send.at[r], far_recv.at[r], (0, 0, r)) for r in range(1, nz)]

    for copy in z_faces:
        copy.wait_recv()
    for px in range(PX):
        for py in range(PY):
            n = px * PY + py
            code_rows[n, 1:5, :] = pad[px, py, 9]
            for side, at_row in ((0, 0), (1, 5)):
                if 1 <= px <= BX and 1 <= py <= BY:
                    i = (px - 1) * BY + py - 1
                    code_rows[n, at_row : at_row + 1, :] = z_own[side, 9, i : i + 1, :]
                else:
                    i = GHOST_COLUMNS.index((px, py))
                    code_rows[n, at_row : at_row + 1, :] = z_ghost[side, 9, i : i + 1, :]
    active = []
    for x in range(BX):
        for y in range(BY):
            listing = jnp.zeros((BZ, SEG), F32)
            for code in range(27):
                if code == 13 or half_shell(code):
                    continue
                ox, oy, oz = step_of(code)
                n = (x + 1 + ox) * PY + y + 1 + oy
                listing = jnp.where(lane == 64 + code, code_rows[n, oz + 1 : oz + 5, :], listing)
            own = jnp.where(lane < 27, pad[x + 1, y + 1, 9], 0.0)
            active.append(own + pltpu.roll(listing, 64, 1) + (lane == 13).astype(F32))
    active = jnp.concatenate(active, axis=0)
    targets = BX * BY * BZ
    before = (iota((SEG, SEG), 0) < iota((SEG, SEG), 1)).astype(BF16)
    rank = jnp.dot(active.astype(BF16), before, preferred_element_type=F32)
    rank = jnp.where(active > 0.5, rank, -1.0)[:, :32]
    totals = jnp.sum(active, axis=1, keepdims=True)
    wide = jnp.broadcast_to(totals, (targets, SEG))
    earlier = (iota((targets, targets), 1) < iota((targets, targets), 0)).astype(BF16)
    base = jnp.dot(earlier, wide.astype(BF16), preferred_element_type=F32)
    end = base + wide
    rank16, names16 = rank.astype(BF16), neighbour_ref[:, :32].astype(BF16)
    contract = (((0,), (0,)), ((), ()))
    target_row = iota((targets, SEG), 0).astype(F32)
    for q in range(LIST_ROWS):
        place = (iota((1, SEG), 1) + q * SEG).astype(F32)
        target = jnp.sum((end <= place).astype(F32), axis=0, keepdims=True)
        chosen = target_row == target
        slot = place - jnp.sum(jnp.where(chosen, base, 0.0), axis=0, keepdims=True)
        chosen16 = chosen.astype(BF16)
        ranks = lax.dot_general(rank16, chosen16, contract, preferred_element_type=F32)
        names = lax.dot_general(names16, chosen16, contract, preferred_element_type=F32)
        source = jnp.sum(jnp.where(ranks == slot, names, 0.0), axis=0, keepdims=True)
        list_ref[q : q + 1, :] = target.astype(jnp.int32)
        list_ref[8 + q : 9 + q, :] = source.astype(jnp.int32)
    list_ref[7:8, :] = end[targets - 1 : targets, :].astype(jnp.int32)
    list_ref[15:16, :] = jnp.zeros((1, SEG), jnp.int32)

    for copy in sent_z:
        copy.wait_recv()
    field = []
    for k in range(2):
        value = sum(table_z[k, r] * got_z[r] for r in range(nz))
        field.append(value + pltpu.roll(value, 6, 0))
    far_ref[...] = exact_dot(jnp.concatenate(field, axis=0), fold_ref[2])

    for copy in faces + z_faces + sent_x + sent_y + sent_z:
        copy.wait_send()


def near_kernel(
    list_ref, far_ref, pad, z_own, z_ghost, node_ref,
    force_out, velocity_out,
    source, target, weigh, gathered, k_rows, q_rows, x_rows, t_rows, place_rows,
):
    row8, lane8 = iota((8, SEG), 0), iota((8, SEG), 1)
    one = jnp.ones((8, SEG), F32)

    def by_row(values):
        if len(set(values)) == 1:
            return float(values[0])
        column = jnp.full((8, SEG), float(values[0]), F32)
        for i in range(1, 8):
            column = jnp.where(row8 >= i, float(values[i]), column)
        return column

    source[...] = jnp.zeros_like(source)
    target[...] = jnp.zeros_like(target)
    gathered[...] = jnp.zeros_like(gathered)
    k_rows[...] = jnp.zeros_like(k_rows)
    q_rows[...] = jnp.zeros_like(q_rows)
    x_rows[...] = jnp.zeros_like(x_rows)
    t_rows[...] = jnp.zeros_like(t_rows)

    def features(step, first, value, shifts, own):
        kept = step % 2
        place = [value[a] + by_row(shifts[a]) for a in range(3)]
        burgers, line = value[3:6], value[6:9]
        product = [[burgers[i] * line[j] for j in range(3)] for i in range(3)]
        coupled = [NEAR_SCALE * (product[i][j] - 2.0 * product[j][i]) for i in range(3) for j in range(3)]
        split = [parts(v, 2) for v in coupled]
        place_parts = [parts(v, 3) for v in place]
        norm = place[0] * place[0] + place[1] * place[1] + place[2] * place[2]
        norm_parts = parts(norm, 3)
        k_feature = [s[0] for s in split] + [s[1] for s in split] + [s[0] for s in split]
        q_feature = [p[i] for i in (0, 1, 0, 2, 0, 1) for p in place_parts] + [one, one, one] + norm_parts
        for i, v in enumerate(k_feature):
            k_rows[kept, pl.ds(i, 8, stride=32), :] = v
        for i, v in enumerate(q_feature):
            q_rows[kept, pl.ds(i, 8, stride=32), :] = v
        x_feature = {0: place_parts[0][0], 1: place_parts[1][0], 2: place_parts[2][0], 3: one,
                     4: place_parts[0][2], 5: place_parts[1][2], 6: place_parts[2][2],
                     8: place_parts[0][1], 9: place_parts[1][1], 10: place_parts[2][1]}
        for i, v in x_feature.items():
            x_rows[kept, pl.ds(i, 8, stride=16), :] = v
        for b in range(8):
            source[first + b, 0:32, 0:SEG] = k_rows[kept, b * 32 : b * 32 + 32, :].astype(BF16)
            source[first + b, 32:64, SEG:] = q_rows[kept, b * 32 : b * 32 + 32, :].astype(BF16)
            x_value = x_rows[kept, b * 16 : b * 16 + 16, :].astype(BF16)
            weigh[first + b, :, 0:SEG] = x_value
            weigh[first + b, :, SEG:] = x_value
        if own is None:
            return
        split = [parts(product[i][j], 2) for i in range(3) for j in range(3)]
        twice = [[-2.0 * p for p in place_parts[a]] for a in range(3)]
        norm_parts = parts(norm + CORE * CORE, 3)
        feature = [s[0] for s in split] * 2 + [s[1] for s in split] + [None] * 5
        feature += [p[i] for i in (0, 0, 1, 0, 2, 1) for p in twice] + norm_parts + [one, one, one]
        for i, v in enumerate(feature):
            if v is not None:
                t_rows[kept, pl.ds(i, 8, stride=64), :] = v
        for b in range(8):
            target[own + b] = jnp.transpose(t_rows[kept, b * 64 : b * 64 + 64, :]).astype(BF16)
        for a in range(3):
            place_rows[own // 8, a] = place[a]

    step = 0
    for px in range(PX):
        for pair, (low, high) in enumerate(Y_PAIRS):
            value = [jnp.concatenate([pad[px, low, c], pad[px, high, c]], axis=0) for c in range(9)]
            shifts = [[px - 1.5] * 8, [low - 2.5] * 4 + [high - 2.5] * 4, [z - 1.5 for z in range(4)] * 2]
            own = ((px - 1) * BY + low - 1) * BZ if 1 <= px <= BX and pair else None
            features(step, (px * 3 + pair) * 8, value, shifts, own)
            step += 1
    for side in range(2):
        value = [z_own[side, c] for c in range(9)]
        shifts = [[n // 4 - 0.5 for n in range(8)], [n % 4 - 1.5 for n in range(8)], [side * 5 - 2.5] * 8]
        features(step, Z_OWN + side * 8, value, shifts, None)
        step += 1
        for half in range(2):
            value = [z_ghost[side, c, half * 8 : half * 8 + 8, :] for c in range(9)]
            columns = GHOST_COLUMNS[half * 8 : half * 8 + 8]
            shifts = [[px - 1.5 for px, _ in columns], [py - 2.5 for _, py in columns], [side * 5 - 2.5] * 8]
            features(step, Z_GHOST + side * 16 + half * 8, value, shifts, None)
            step += 1

    transposed = (((1,), (1,)), ((), ()))
    per_row = SEG // CHUNK

    def chunk(i, carry):
        list_row, start = i // per_row, lax.rem(i, per_row) * CHUNK
        found = []
        for j in range(CHUNK):
            t, s = list_ref[list_row, start + j], list_ref[8 + list_row, start + j]
            both = jnp.dot(target[t], source[s], preferred_element_type=F32)
            inverse = lax.rsqrt(both[:, SEG:])
            square = inverse * inverse
            weight = (both[:, :SEG] * inverse) * (square * (1.0 + 1.5 * CORE * CORE * square))
            high = weight.astype(BF16)
            low = (weight - high.astype(F32)).astype(BF16)
            halves = jnp.concatenate([high, low], axis=1)
            found.append((t, lax.dot_general(weigh[s], halves, transposed, preferred_element_type=F32)))
        for t, value in found:
            at = pl.multiple_of(t * 16, 16)
            gathered[pl.ds(at, 16), :] += value
        return carry

    lax.fori_loop(0, (list_ref[7, 0] + CHUNK - 1) // CHUNK, chunk, 0)

    for group in range(4):
        x, y = group // 2, group % 2 * 2
        first = group * 8

        def strided(r):
            return gathered[pl.ds(first * 16 + r, 8, stride=16), :]

        weights = strided(3)
        own = [jnp.concatenate([pad[x + 1, y + 1, c], pad[x + 1, y + 2, c]], axis=0) for c in range(3, 10)]
        burgers, line, count = own[0:3], own[3:6], own[6][:, 127:128]
        force = []
        for d in range(3):
            value = (strided(d) + strided(8 + d) + strided(4 + d)) - place_rows[group, d] * weights
            x_row, kind = (0, 0) if d == 0 else (1, 1 if d == 1 else 0)
            for c in range(3):
                at = [far_ref[k * 8 + group % 2 * 4 + x_row, kind * 3 + c] for k in range(2)]
                value += jnp.where(row8 % 4 < 2, at[0], at[1]) * burgers[c]
            force.append(value)
            force_out[x, y, d] = value[0:4]
            force_out[x, y + 1, d] = value[4:8]
        nodes = [
            jnp.concatenate([node_ref[x, y, :, i, :], node_ref[x, y + 1, :, i, :]], axis=0) for i in range(2)
        ]

        def take(v, i):
            return jnp.take_along_axis(v, nodes[i], axis=1)

        node_force = [0.5 * (take(v, 0) + take(v, 1)) for v in force]
        b, t = [take(v, 0) for v in burgers], [take(v, 0) for v in line]
        normal = [t[1] * b[2] - t[2] * b[1], t[2] * b[0] - t[0] * b[2], t[0] * b[1] - t[1] * b[0]]
        along = node_force[0] * normal[0] + node_force[1] * normal[1] + node_force[2] * normal[2]
        size = jnp.maximum(normal[0] * normal[0] + normal[1] * normal[1] + normal[2] * normal[2], 1.0)
        ratio = (1.0 - CLIMB) * along / size
        live = lane8.astype(F32) < count
        for d in range(3):
            value = jnp.where(live, node_force[d] - ratio * normal[d], 0.0)
            velocity_out[x, y, d] = value[0:4]
            velocity_out[x, y + 1, d] = value[4:8]


def local(sizes, segments, seg_count, pair_offsets, pair_count, node_segs):
    nx, ny, nz = sizes
    by_component = jnp.transpose(segments, (0, 1, 3, 2, 4))
    table_x, table_y, table_z, fold = far_tables(nx, ny, nz)
    vmem, smem = pl.BlockSpec(memory_space=pltpu.VMEM), pl.BlockSpec(memory_space=pltpu.SMEM)
    dma = pltpu.SemaphoreType.DMA
    pad, z_own, z_ghost, tiles, far = pl.pallas_call(
        functools.partial(exchange_kernel, sizes),
        out_shape=(
            jax.ShapeDtypeStruct((PX, PY, COMPS, BZ, SEG), F32),
            jax.ShapeDtypeStruct((2, COMPS, 8, SEG), F32),
            jax.ShapeDtypeStruct((2, COMPS, 16, SEG), F32),
            jax.ShapeDtypeStruct((16, SEG), jnp.int32),
            jax.ShapeDtypeStruct((16, SEG), F32),
        ),
        in_specs=[vmem] * 9,
        out_specs=(vmem,) * 5,
        scratch_shapes=[
            pltpu.VMEM((2, COMPS, 8, SEG), F32),
            pltpu.VMEM((2, COMPS, 16, SEG), F32),
            pltpu.VMEM((nx, 8, SEG), F32),
            pltpu.VMEM((ny, 8, SEG), F32),
            pltpu.VMEM((nz, 8, SEG), F32),
            pltpu.VMEM((PX * PY, 8, SEG), F32),
            dma((8,)), dma((8,)), dma((4,)), dma((4,)),
            dma((nx,)), dma((nx,)), dma((ny,)), dma((ny,)), dma((nz,)), dma((nz,)),
        ],
        compiler_params=pltpu.CompilerParams(collective_id=0, has_side_effects=True, vmem_limit_bytes=24 << 20),
        name="exchange",
    )(
        by_component, seg_count, pair_offsets, pair_count,
        table_x, table_y, table_z, jnp.asarray(fold, BF16), neighbour_table(),
    )
    force, velocity = pl.pallas_call(
        near_kernel,
        out_shape=(jax.ShapeDtypeStruct((BX, BY, 3, BZ, SEG), F32),) * 2,
        in_specs=[smem, smem] + [vmem] * 4,
        out_specs=(vmem, vmem),
        scratch_shapes=[
            pltpu.VMEM((BLOCKS, 64, 2 * SEG), BF16),
            pltpu.VMEM((BX * BY * BZ + 1, SEG, 64), BF16),
            pltpu.VMEM((BLOCKS, 16, 2 * SEG), BF16),
            pltpu.VMEM(((BX * BY * BZ + 1) * 16, SEG), F32),
            pltpu.VMEM((2, 8 * 32, SEG), F32),
            pltpu.VMEM((2, 8 * 32, SEG), F32),
            pltpu.VMEM((2, 8 * 16, SEG), F32),
            pltpu.VMEM((2, 8 * 64, SEG), F32),
            pltpu.VMEM((4, 3, 8, SEG), F32),
        ],
        compiler_params=pltpu.CompilerParams(vmem_limit_bytes=40 << 20),
        name="near",
    )(tiles, far, pad, z_own, z_ghost, node_segs)
    return tuple(jnp.transpose(v, (0, 1, 3, 2, 4)) for v in (force, velocity))


def solution(mesh):
    sizes = tuple(mesh.shape[axis] for axis in ("gx", "gy", "gz"))
    placed = (
        P("gx", "gy", "gz", None, None),
        P("gx", "gy", "gz"),
        P("gx", "gy", "gz", None),
        P("gx", "gy", "gz"),
        P("gx", "gy", "gz", None, None),
    )
    return jax.shard_map(
        functools.partial(local, sizes),
        mesh=mesh,
        in_specs=placed,
        out_specs=(P("gx", "gy", "gz", None, None), P("gx", "gy", "gz", None, None)),
        check_vma=False,
    )
```

time: 378 us -> 63.3 us (0.17)
  the two profiles are of different devices: /device:TPU:1 before, /device:TPU:24 now
where the time goes in v1:
time: 63.3 us; the launch traced here: 62.8 us
  Pallas kernels  55.1 us (87%)
  local copies, waits for them, and re-layouts  7.04 us (11%)
  between operations  0.66 us (1%)
    pallas_call x1, Pallas kernels, local(): pl.pallas_call(functools.partial(exchange_kernel, sizes), out_shape=(jax....  30.4 us
    pallas_call x1, Pallas kernels, local(): pl.pallas_call(near_kernel, out_shape=(jax.ShapeDtypeStruct((BX, BY, 3, B...  24.6 us
    unnamed x20, local copies, waits for them, and re-layouts  7.04 us

profile of v1, /device:TPU:24, one launch (start us, length us, event | category | flops | bytes accessed | tf_op | source)
XLA Modules:
  0.0 62.8 jit_solution(8179807969300037506)
XLA Ops:
  0.6 0.0 copy-start
  0.6 0.9 %copy-done = f32[2,4,4,9,128]{4,2,3,1,0:T(4,128)S(1)} copy-done((f32[2,4,4,9,128]{4,2,3,1,0:T(4,128)S(1)}, f32[2,4,4,9,128]{4,2,3,1,0:T(4,128)}, u32[]{:S(2)}) %copy-start) | copy-done | bytes 147480
  1.5 0.0 copy-start.1
  1.5 0.9 %copy-done.1 = f32[2,16,8,128]{3,2,1,0:T(8,128)S(1)} copy-done((f32[2,16,8,128]{3,2,1,0:T(8,128)S(1)}, f32[2,16,8,128]{3,2,1,0:T(8,128)}, u32[]{:S(2)}) %copy-start.1) | copy-done | bytes 131096
  2.4 0.0 copy-start.2
  2.4 0.9 %copy-done.2 = bf16[3,128,128]{2,1,0:T(8,128)(2,1)S(1)} copy-done((bf16[3,128,128]{2,1,0:T(8,128)(2,1)S(1)}, bf16[3,128,128]{2,1,0:T(8,128)(2,1)}, u32[]{:S(2)}) %copy-start.2) | copy-done | bytes 98328
  3.3 0.0 copy-start.3
  3.3 0.8 %copy-done.3 = f32[2,2,4,8,128]{4,3,2,1,0:T(8,128)S(1)} copy-done((f32[2,2,4,8,128]{4,3,2,1,0:T(8,128)S(1)}, f32[2,2,4,8,128]{4,3,2,1,0:T(8,128)}, u32[]{:S(2)}) %copy-start.3) | copy-done | bytes 65560
  4.2 0.0 copy-start.5
  4.2 0.7 %copy-done.5 = s32[2,4,4,13]{3,2,1,0:T(4,128)S(1)} copy-done((s32[2,4,4,13]{3,2,1,0:T(4,128)S(1)}, s32[2,4,4,13]{3,2,1,0:T(4,128)}, u32[]{:S(2)}) %copy-start.5) | copy-done | bytes 1688
  4.9 0.0 copy-start.6
  4.9 0.7 %copy-done.6 = f32[32,128]{1,0:T(8,128)S(1)} copy-done((f32[32,128]{1,0:T(8,128)S(1)}, f32[32,128]{1,0:T(8,128)}, u32[]{:S(2)}) %copy-start.6) | copy-done | bytes 16408
  5.6 0.0 copy-start.7
  5.6 0.7 %copy-done.7 = f32[2,8,128]{2,1,0:T(8,128)S(1)} copy-done((f32[2,8,128]{2,1,0:T(8,128)S(1)}, f32[2,8,128]{2,1,0:T(8,128)}, u32[]{:S(2)}) %copy-start.7) | copy-done | bytes 8216
  6.3 0.0 copy-start.8
  6.3 0.7 %copy-done.8 = s32[2,4,4]{2,1,0:T(4,128)S(1)} copy-done((s32[2,4,4]{2,1,0:T(4,128)S(1)}, s32[2,4,4]{2,1,0:T(4,128)}, u32[]{:S(2)}) %copy-start.8) | copy-done | bytes 152
  7.0 0.0 copy-start.9
  7.0 0.7 %copy-done.9 = s32[2,4,4]{2,1,0:T(4,128)S(1)} copy-done((s32[2,4,4]{2,1,0:T(4,128)S(1)}, s32[2,4,4]{2,1,0:T(4,128)}, u32[]{:S(2)}) %copy-start.9) | copy-done | bytes 152
  7.7 0.0 copy-start.4
  7.7 30.4 %exchange.1 = (f32[4,6,10,4,128]{4,3,2,1,0:T(4,128)S(1)}, f32[2,10,8,128]{3,2,1,0:T(8,128)S(1)}, f32[2,10,16,128]{3,2,1,0:T(8,128)S(1)}, s32[16,128]{1,0:T(8,128)S(1)}, f32[16,128]{1,0:T(8,128)S(1)}) custom-call(f32[2,4,9,4,128]{4,3,2,1,0:T(4,128)S(1)} %bitcast.3, s32[2,4,4]{2,1,0:T(4,128)S(1)} %copy-done.8, s32[2,4,4,13]{3,2,1,0:T(4,128)S(1)} %copy-done.5, ...), custom_call_target="tpu_custom_call" | custom-call | tf_op jit(solution)/shard_map/exchange/pallas_call | solution.py:506
  38.1 0.0 copy-done.4
  38.1 24.6 %near.1 = (f32[2,4,3,4,128]{4,3,2,1,0:T(4,128)}, f32[2,4,3,4,128]{4,3,2,1,0:T(4,128)}) custom-call(s32[16,128]{1,0:T(8,128)S(1)} %get-tuple-element.9.list_ref, f32[16,128]{1,0:T(8,128)S(1)} %get-tuple-element.10.far_ref, f32[4,6,10,4,128]{4,3,2,1,0:T(4,128)S(1)} %get-tuple-element.11.pad, f32[2,10,8,128]{3,2,1,0:T(8,128)S(1)} %get-tuple-element.12.z_own, ...), custom_call_target="tpu_custom_call" | custom-call | tf_op jit(solution)/shard_map/near/pallas_call | solution.py:533
Async XLA Ops:
  0.6 0.9 %copy-start = (f32[2,4,4,9,128]{4,2,3,1,0:T(4,128)S(1)}, f32[2,4,4,9,128]{4,2,3,1,0:T(4,128)}, u32[]{:S(2)}) copy-start(f32[2,4,4,9,128]{4,2,3,1,0:T(4,128)} %param.10) | copy-start | bytes 442372
  1.5 0.9 %copy-start.1 = (f32[2,16,8,128]{3,2,1,0:T(8,128)S(1)}, f32[2,16,8,128]{3,2,1,0:T(8,128)}, u32[]{:S(2)}) copy-start(f32[2,16,8,128]{3,2,1,0:T(8,128)} %constant.13.clone.table_z) | copy-start | bytes 393220
  2.4 0.9 %copy-start.2 = (bf16[3,128,128]{2,1,0:T(8,128)(2,1)S(1)}, bf16[3,128,128]{2,1,0:T(8,128)(2,1)}, u32[]{:S(2)}) copy-start(bf16[3,128,128]{2,1,0:T(8,128)(2,1)} %constant.10.clone.fold_ref) | copy-start | bytes 294916
  3.3 0.8 %copy-start.3 = (f32[2,2,4,8,128]{4,3,2,1,0:T(8,128)S(1)}, f32[2,2,4,8,128]{4,3,2,1,0:T(8,128)}, u32[]{:S(2)}) copy-start(f32[2,2,4,8,128]{4,3,2,1,0:T(8,128)} %constant.12.clone.table_y) | copy-start | bytes 196612
  4.2 0.7 %copy-start.5 = (s32[2,4,4,13]{3,2,1,0:T(4,128)S(1)}, s32[2,4,4,13]{3,2,1,0:T(4,128)}, u32[]{:S(2)}) copy-start(s32[2,4,4,13]{3,2,1,0:T(4,128)} %offset_ref.1) | copy-start | bytes 4996
  4.9 0.7 %copy-start.6 = (f32[32,128]{1,0:T(8,128)S(1)}, f32[32,128]{1,0:T(8,128)}, u32[]{:S(2)}) copy-start(f32[32,128]{1,0:T(8,128)} %constant.14.clone.neighbour_ref) | copy-start | bytes 49156
  5.6 0.7 %copy-start.7 = (f32[2,8,128]{2,1,0:T(8,128)S(1)}, f32[2,8,128]{2,1,0:T(8,128)}, u32[]{:S(2)}) copy-start(f32[2,8,128]{2,1,0:T(8,128)} %constant.11.clone.table_x) | copy-start | bytes 24580
  6.3 0.7 %copy-start.8 = (s32[2,4,4]{2,1,0:T(4,128)S(1)}, s32[2,4,4]{2,1,0:T(4,128)}, u32[]{:S(2)}) copy-start(s32[2,4,4]{2,1,0:T(4,128)} %count_ref.1) | copy-start | bytes 388
  7.0 0.7 %copy-start.9 = (s32[2,4,4]{2,1,0:T(4,128)S(1)}, s32[2,4,4]{2,1,0:T(4,128)}, u32[]{:S(2)}) copy-start(s32[2,4,4]{2,1,0:T(4,128)} %pair_count_ref.1) | copy-start | bytes 388
  7.7 30.4 %copy-start.4 = (s32[2,4,4,2,128]{4,3,2,1,0:T(2,128)S(1)}, s32[2,4,4,2,128]{4,3,2,1,0:T(2,128)}, u32[]{:S(2)}) copy-start(s32[2,4,4,2,128]{4,3,2,1,0:T(2,128)} %node_ref.1) | copy-start | bytes 98308

commit v2 on v1

v2 whole, which is shorter than its diff:
```python
import functools
import math

import jax
import jax.numpy as jnp
import numpy as np
from jax import lax
from jax.experimental import pallas as pl
from jax.experimental.pallas import tpu as pltpu
from jax.sharding import PartitionSpec as P

CORE = 0.3
NEAR_SCALE = 0.02
FAR_SCALE = 0.05
LENGTH = 1.5
CLIMB = 0.1
SQUARE_SCALE = 1.0 / (1.5 * CORE * CORE)
PAIR_SCALE = NEAR_SCALE * SQUARE_SCALE**1.5

MESH = pl.DeviceIdType.MESH
F32 = jnp.float32
BF16 = jnp.bfloat16

BX, BY, BZ, SEG = 2, 4, 4, 128
PX, PY = BX + 2, BY + 2
COMPS = 10
PAIRS = 13
CHUNK = 32
VMEM_LIMIT = 63 << 20
LIST_ROWS = 7
EARLY = (64, 64, 64)
EARLY_ALL = sum(EARLY)

GHOST_COLUMNS = (
    [(0, py) for py in range(PY)]
    + [(PX - 1, py) for py in range(PY)]
    + [(px, py) for px in (1, 2) for py in (0, PY - 1)]
)
OWN = BX * BY * BZ
COLUMN_GHOST = OWN
Z_OWN = COLUMN_GHOST + len(GHOST_COLUMNS) * BZ
Z_GHOST = Z_OWN + 2 * BX * BY
BLOCKS = Z_GHOST + 2 * len(GHOST_COLUMNS)


def block_index(px, py, pz):
    own_column = 1 <= px <= BX and 1 <= py <= BY
    if 1 <= pz <= BZ:
        if own_column:
            return ((px - 1) * BY + py - 1) * BZ + pz - 1
        return COLUMN_GHOST + GHOST_COLUMNS.index((px, py)) * BZ + pz - 1
    side = 0 if pz == 0 else 1
    if own_column:
        return Z_OWN + side * 8 + (px - 1) * BY + py - 1
    return Z_GHOST + side * 16 + GHOST_COLUMNS.index((px, py))


def step_of(code):
    return code // 9 - 1, code // 3 % 3 - 1, code % 3 - 1


def half_shell(code):
    total = sum(step_of(code))
    return total > 0 or (total == 0 and code > 13)


def neighbour_table():
    table = np.zeros((2, OWN, 128), np.float32)
    for x in range(BX):
        for y in range(BY):
            for z in range(BZ):
                for code in range(27):
                    ox, oy, oz = step_of(code)
                    name = block_index(x + 1 + ox, y + 1 + oy, z + 1 + oz)
                    table[:, (x * BY + y) * BZ + z, code] = name, name < OWN
    return table


def exponents():
    rows = []
    for degree in range(5):
        for power_x in range(degree, -1, -1):
            for power_y in range(degree - power_x, -1, -1):
                rows.append((power_x, power_y, degree - power_x - power_y))
    return rows


def axis_values(total):
    units = np.arange(total)
    radius = 2.0 * (((units + total // 2) % total) - total // 2).astype(np.float64)
    scale = 1.0 / LENGTH**2
    base = 1.0 + scale * radius**2
    poly = np.polynomial.Polynomial([1.0])
    derivatives = []
    for order in range(6):
        derivatives.append(poly(radius) * base ** (-(2 * order + 1) / 2))
        poly = poly.deriv() * np.polynomial.Polynomial([1.0, 0.0, scale]) - np.polynomial.Polynomial(
            [0.0, (2 * order + 1) * scale]
        ) * poly
    factor = [(-1.0) ** n / math.factorial(n) for n in range(5)]
    g = np.stack([factor[n] * derivatives[n] for n in range(5)])
    h = np.stack([factor[n] * derivatives[n + 1] for n in range(5)])
    return g, h


def far_tables(nx, ny, nz):
    powers = exponents()
    table_x = np.zeros((2, nx, 128))
    values = axis_values(nx)
    for kind in range(2):
        for r in range(nx):
            for c in range(3):
                for p, power in enumerate(powers):
                    table_x[kind, r, c * 35 + p] = values[kind][power[0], r % nx]
    table_y = np.zeros((2, 2, ny, 8, 128))
    total = 2 * ny
    values = axis_values(total)
    for kind in range(2):
        for j in range(2):
            for r in range(ny):
                for row in range(8):
                    unit = (2 * r + j - row // 4) % total
                    for c in range(3):
                        for p, power in enumerate(powers):
                            table_y[kind, j, r, row, c * 35 + p] = values[kind][power[1], unit]
    table_z = np.zeros((2, nz, 8, 128))
    total = 2 * nz
    values = axis_values(total)
    for k in range(2):
        for r in range(nz):
            for row in range(8):
                unit = (2 * r + k - row // 2 % 2) % total
                x_kind = 1 - row % 2
                for y_kind in range(2):
                    z_kind = 1 if (x_kind == 0 and y_kind == 0) else 0
                    for c in range(3):
                        for n in range(5):
                            lane = y_kind * 16 + c * 5 + n
                            table_z[k, r, row, lane] = -FAR_SCALE * values[z_kind][n, unit]
    fold = np.zeros((3, 128, 128))
    for c in range(3):
        for p, power in enumerate(powers):
            for kind in range(2):
                fold[kind, c * 35 + p, kind * 16 + c * 5 + power[2]] = 1.0
        for n in range(5):
            for kind in range(2):
                fold[2, kind * 16 + c * 5 + n, kind * 3 + c] = 1.0
    return [a.astype(np.float32) for a in (table_x, table_y, table_z, fold)]


def iota(shape, dim):
    return lax.broadcasted_iota(jnp.int32, shape, dim)


def parts(value, count):
    found = []
    for _ in range(count):
        part = value.astype(BF16).astype(F32)
        found.append(part)
        value = value - part
    return found


def exact_dot(value, zero_one):
    return sum(jnp.dot(p.astype(BF16), zero_one, preferred_element_type=F32) for p in parts(value, 3))


def by_row(values):
    if len(set(values)) == 1:
        return float(values[0])
    rows = iota((8, SEG), 0)
    column = jnp.full((8, SEG), float(values[0]), F32)
    for i in range(1, 8):
        if values[i] != values[i - 1]:
            column = jnp.where(rows >= i, float(values[i]), column)
    return column


def features(step, first, value, shifts, source, weigh, rows, own=None):
    k_rows, q_rows, x_rows = rows
    kept = step % 2
    one = jnp.ones((8, SEG), F32)
    empty = jnp.zeros((32, SEG), BF16)
    place = [value[a] + by_row(shifts[a]) for a in range(3)]
    burgers, line = value[3:6], value[6:9]
    product = [[burgers[i] * line[j] for j in range(3)] for i in range(3)]
    coupled = [PAIR_SCALE * (product[i][j] - 2.0 * product[j][i]) for i in range(3) for j in range(3)]
    split = [parts(v, 2) for v in coupled]
    place_parts = [parts(v, 3) for v in place]
    scaled = [parts(v * SQUARE_SCALE, 3) for v in place]
    norm = (place[0] * place[0] + place[1] * place[1] + place[2] * place[2]) * SQUARE_SCALE
    norm_parts = parts(norm, 3)
    k_feature = [s[0] for s in split] + [s[1] for s in split] + [s[0] for s in split]
    q_feature = [p[i] for i in (0, 1, 0, 2, 0, 1) for p in scaled] + [one, one, one] + norm_parts
    for i, v in enumerate(k_feature):
        k_rows[kept, pl.ds(i, 8, stride=32), :] = v
    for i, v in enumerate(q_feature):
        q_rows[kept, pl.ds(i, 8, stride=32), :] = v
    x_feature = {0: place_parts[0][0], 1: place_parts[1][0], 2: place_parts[2][0], 3: one,
                 4: place_parts[0][2], 5: place_parts[1][2], 6: place_parts[2][2],
                 8: place_parts[0][1], 9: place_parts[1][1], 10: place_parts[2][1]}
    for i, v in x_feature.items():
        x_rows[kept, pl.ds(i, 8, stride=16), :] = v
    for b in range(8):
        source[first + b, 0:32, 0:SEG] = k_rows[kept, b * 32 : b * 32 + 32, :].astype(BF16)
        source[first + b, 0:32, SEG:] = empty
        source[first + b, 32:64, 0:SEG] = empty
        source[first + b, 32:64, SEG:] = q_rows[kept, b * 32 : b * 32 + 32, :].astype(BF16)
        x_value = x_rows[kept, b * 16 : b * 16 + 16, :].astype(BF16)
        weigh[first + b, :, 0:SEG] = x_value
        weigh[first + b, :, SEG:] = x_value
    if own is None:
        return
    target, t_rows, place_rows = own
    split = [parts(product[i][j], 2) for i in range(3) for j in range(3)]
    twice = [[-2.0 * p for p in place_parts[a]] for a in range(3)]
    norm_parts = parts(norm + CORE * CORE * SQUARE_SCALE, 3)
    feature = [s[0] for s in split] * 2 + [s[1] for s in split] + [None] * 5
    feature += [p[i] for i in (0, 0, 1, 0, 2, 1) for p in twice] + norm_parts + [one, one, one]
    for i, v in enumerate(feature):
        if v is not None:
            t_rows[kept, pl.ds(i, 8, stride=64), :] = v
    for b in range(8):
        target[first + b] = jnp.transpose(t_rows[kept, b * 64 : b * 64 + 64, :]).astype(BF16)
    for a in range(3):
        place_rows[first // 8, a] = place[a]


def near_tiles(chosen, target, source, weigh):
    transposed = (((1,), (1,)), ((), ()))
    count, lead = len(chosen), 4
    both, halves, found = {}, {}, []
    for step in range(count + 2 * lead):
        if step < count:
            t, s = chosen[step]
            both[step] = jnp.dot(target[t], source[s], preferred_element_type=F32)
        if 0 <= step - lead < count:
            value = both.pop(step - lead)
            inverse = lax.rsqrt(value[:, SEG:])
            square = inverse * inverse
            weight = (value[:, :SEG] * inverse) * (square * (square + 1.0))
            high = weight.astype(BF16)
            low = (weight - high.astype(F32)).astype(BF16)
            halves[step - lead] = jnp.concatenate([high, low], axis=1)
        if 0 <= step - 2 * lead < count:
            i = step - 2 * lead
            total = lax.dot_general(weigh[chosen[i][1]], halves.pop(i), transposed, preferred_element_type=F32)
            found.append(total[0:8] + total[8:16])
    return found


def listed_tiles(active, names, list_rows, gap=0.0):
    rows = active.shape[0]
    before = (iota((SEG, SEG), 0) < iota((SEG, SEG), 1)).astype(BF16)
    rank = jnp.dot(active.astype(BF16), before, preferred_element_type=F32)
    rank = jnp.where(active > 0.5, rank, -1.0)[:, :32].astype(BF16)
    names = names[:, :32].astype(BF16)
    wide = jnp.broadcast_to(jnp.sum(active, axis=1, keepdims=True), (rows, SEG))
    earlier = (iota((rows, rows), 1) < iota((rows, rows), 0)).astype(BF16)
    row = iota((rows, SEG), 0).astype(F32)
    base = jnp.dot(earlier, wide.astype(BF16), preferred_element_type=F32)
    base += jnp.where(row < OWN, 0.0, gap)
    end = base + wide
    contract = (((0,), (0,)), ((), ()))
    found = []
    for q in range(list_rows):
        place = (iota((1, SEG), 1) + q * SEG).astype(F32)
        owner = jnp.sum((end <= place).astype(F32), axis=0, keepdims=True)
        chosen = row == owner
        slot = place - jnp.sum(jnp.where(chosen, base, 0.0), axis=0, keepdims=True)
        chosen = chosen.astype(BF16)
        ranks = lax.dot_general(rank, chosen, contract, preferred_element_type=F32)
        called = lax.dot_general(names, chosen, contract, preferred_element_type=F32)
        found.append((owner, jnp.sum(jnp.where(ranks == slot, called, 0.0), axis=0, keepdims=True)))
    return found, end[rows - 1 : rows, :]


def exchange_kernel(
    sizes,
    seg_hbm, count_hbm, offset_hbm, pair_count_hbm, table_x_hbm, table_y_hbm, table_z_hbm, fold_hbm, neighbour_hbm,
    pad_out, z_own_out, z_ghost_out, list_out, far_out, source_out, weigh_out, target_out, place_out, early_out,
    pad, z_own, z_ghost, list_ref, far_ref, source, weigh, target, place_rows, early,
    seg_ref, count_ref, offset_ref, pair_count_ref, table_x, table_y, table_z, fold_ref, neighbour_ref,
    own_face, ghost_face, got_x, got_y, got_z, code_rows, k_rows, q_rows, x_rows, t_rows, early_list, early_smem,
    in_sem, out_sem, smem_sem, face_send, face_recv, z_send, z_recv, x_send, x_recv, y_send, y_recv, far_send, far_recv,
):
    nx, ny, nz = sizes
    gx, gy, gz = lax.axis_index("gx"), lax.axis_index("gy"), lax.axis_index("gz")

    def at(dx, dy, dz):
        return (lax.rem(gx + dx + nx, nx), lax.rem(gy + dy + ny, ny), lax.rem(gz + dz + nz, nz))

    loads = []
    for i, (src, dst) in enumerate((
        (seg_hbm, seg_ref), (count_hbm, count_ref), (offset_hbm, offset_ref), (pair_count_hbm, pair_count_ref),
        (neighbour_hbm, neighbour_ref), (table_x_hbm, table_x), (table_y_hbm, table_y), (table_z_hbm, table_z),
        (fold_hbm, fold_ref),
    )):
        loads.append(pltpu.make_async_copy(src, dst, in_sem.at[i]))
        loads[-1].start()

    peers = [(r, 0, 0) for r in range(1, nx)] + [(0, r, 0) for r in range(1, ny)] + [(0, 0, r) for r in range(1, nz)]
    peers += [(dx, dy, 0) for dx in (-1, 1) for dy in (-1, 1)]
    barrier = pltpu.get_barrier_semaphore()
    for peer in peers:
        pl.semaphore_signal(barrier, inc=1, device_id=at(*peer), device_id_type=MESH)

    def send(src, dst, send_sem, recv_sem, peer):
        copy = pltpu.make_async_remote_copy(
            src_ref=src, dst_ref=dst, send_sem=send_sem, recv_sem=recv_sem, device_id=at(*peer), device_id_type=MESH
        )
        copy.start()
        return copy

    for ref in (k_rows, q_rows, x_rows, t_rows, code_rows):
        ref[...] = jnp.zeros_like(ref)
    target[OWN] = jnp.zeros((SEG, 64), BF16)
    for copy in loads:
        copy.wait()

    lane = iota((BZ, SEG), 1)
    row = iota((BZ, SEG), 0)
    row8, lane8 = iota((8, SEG), 0), iota((8, SEG), 1)

    def column(ref, x, y):
        found = [
            jnp.sum(jnp.where(lane[:, :BZ] == row[:, :BZ], ref[x, v : v + 1, :], 0), axis=1, keepdims=True)
            for v in (y, y + 1)
        ]
        return jnp.concatenate(found, axis=0)

    for x in range(BX):
        for y in range(0, BY, 2):
            count = column(count_ref, x, y)
            live = lane8 < count
            for c in range(9):
                value = jnp.concatenate([seg_ref[x, y, c], seg_ref[x, y + 1, c]], axis=0)
                value = value if c < 3 else jnp.where(live, value, 0.0)
                pad[x + 1, y + 1, c] = value[0:4]
                pad[x + 1, y + 2, c] = value[4:8]
            listed = column(pair_count_ref, x, y)
            offsets = jnp.concatenate([offset_ref[x, y], offset_ref[x, y + 1]], axis=0)
            codes = jnp.where(lane8 == 127, count, 0)
            for i in range(PAIRS):
                code = jnp.where(i < listed, offsets[:, i : i + 1], -64)
                codes = jnp.where((lane8 == code) | (lane8 == 90 - code), 1, codes)
            codes = codes.astype(F32)
            pad[x + 1, y + 1, 9] = codes[0:4]
            pad[x + 1, y + 2, 9] = codes[4:8]
    for side, z in ((0, 0), (1, BZ - 1)):
        for c in range(COMPS):
            for x in range(BX):
                for y in range(BY):
                    own_face[side, c, x * BY + y : x * BY + y + 1, :] = pad[x + 1, y + 1, c, z : z + 1, :]

    z_part = (row8 % 2).astype(F32) - 0.5
    powers = exponents()
    totals = None
    for x in range(BX):
        for parity in range(2):
            value = [
                jnp.concatenate([pad[x + 1, parity + 1, c], pad[x + 1, parity + 3, c]], axis=0) for c in range(6)
            ]
            at_x, at_y, at_z = value[0] + (x - 0.5), value[1] + (parity - 0.5), value[2] + z_part
            mono = {}
            for power in powers:
                if sum(power) == 0:
                    continue
                axis = next(a for a in range(3) if power[a])
                lower = tuple(n - (a == axis) for a, n in enumerate(power))
                factor = (at_x, at_y, at_z)[axis]
                mono[power] = factor if sum(lower) == 0 else mono[lower] * factor
            terms = [
                value[3 + c] if sum(power) == 0 else mono[power] * value[3 + c] for c in range(3) for power in powers
            ]
            totals = terms if totals is None else [a + b for a, b in zip(totals, terms)]
    moments = jnp.zeros((8, SEG), F32)
    for i, term in enumerate(totals):
        moments = jnp.where(lane8 == i, jnp.sum(term, axis=1, keepdims=True), moments)
    got_x[0] = moments

    pl.semaphore_wait(barrier, len(peers))

    sent_x = [send(got_x.at[0], got_x.at[r], x_send.at[r], x_recv.at[r], (r, 0, 0)) for r in range(1, nx)]
    faces = []
    moves = [(1, 0, pad.at[2, 1:5], pad.at[0, 1:5]), (-1, 0, pad.at[1, 1:5], pad.at[3, 1:5]),
             (0, 1, pad.at[1:3, 4], pad.at[1:3, 0]), (0, -1, pad.at[1:3, 1], pad.at[1:3, 5])]
    for dx in (-1, 1):
        for dy in (-1, 1):
            moves.append((dx, dy, pad.at[2 if dx > 0 else 1, 4 if dy > 0 else 1], pad.at[0 if dx > 0 else 3, 0 if dy > 0 else 5]))
    for i, (dx, dy, src, dst) in enumerate(moves):
        faces.append(send(src, dst, face_send.at[i], face_recv.at[i], (dx, dy, 0)))
    z_faces = [
        send(own_face.at[0], z_own.at[1], z_send.at[0], z_recv.at[0], (0, 0, -1)),
        send(own_face.at[1], z_own.at[0], z_send.at[1], z_recv.at[1], (0, 0, 1)),
    ]

    for x in range(BX):
        for y in range(0, BY, 2):
            value = [jnp.concatenate([pad[x + 1, y + 1, c], pad[x + 1, y + 2, c]], axis=0) for c in range(9)]
            shifts = [[x - 0.5] * 8, [y - 1.5] * 4 + [y - 0.5] * 4, [z - 1.5 for z in range(4)] * 2]
            features(x * 2 + y // 2, (x * BY + y) * BZ, value, shifts, source, weigh, (k_rows, q_rows, x_rows),
                     (target, t_rows, place_rows))

    stores = []

    def store(*pairs):
        for src, dst in pairs:
            stores.append(pltpu.make_async_copy(src, dst, out_sem.at[len(stores)]))
            stores[-1].start()

    store((source, source_out), (weigh, weigh_out), (target, target_out), (place_rows, place_out))

    def active_codes():
        active = []
        for x in range(BX):
            for y in range(BY):
                listing = jnp.zeros((BZ, SEG), F32)
                for code in range(27):
                    if code == 13 or half_shell(code):
                        continue
                    ox, oy, oz = step_of(code)
                    n = (x + 1 + ox) * PY + y + 1 + oy
                    listing = jnp.where(lane == 64 + code, code_rows[n, oz + 1 : oz + 5, :], listing)
                own = jnp.where(lane < 27, pad[x + 1, y + 1, 9], 0.0)
                active.append(own + pltpu.roll(listing, 64, 1) + (lane == 13).astype(F32))
        return jnp.concatenate(active, axis=0)

    for x in range(1, BX + 1):
        for y in range(1, BY + 1):
            code_rows[x * PY + y, 1:5, :] = pad[x, y, 9]
    names, inside = neighbour_ref[0], neighbour_ref[1]
    active_inside = active_codes() * inside
    early_found, early_total = listed_tiles(active_inside, names, 2)
    early_list[...] = jnp.zeros_like(early_list)
    for q, (owner, name) in enumerate(early_found):
        early_list[q : q + 1, :] = owner.astype(jnp.int32)
        early_list[4 + q : 5 + q, :] = name.astype(jnp.int32)
    to_smem = pltpu.make_async_copy(early_list, early_smem, smem_sem)
    to_smem.start()
    to_smem.wait()

    def early_run(first, count):
        def chunk(i, carry):
            list_row, start = i // (SEG // CHUNK), lax.rem(i, SEG // CHUNK) * CHUNK
            chosen = [
                (
                    jnp.clip(early_smem[list_row, start + j], 0, OWN),
                    jnp.clip(early_smem[4 + list_row, start + j], 0, OWN - 1),
                )
                for j in range(CHUNK)
            ]
            for j, value in enumerate(near_tiles(chosen, target, source, weigh)):
                early[i * CHUNK + j] = value
            return carry

        lax.fori_loop(first // CHUNK, (first + count) // CHUNK, chunk, 0)

    early_run(0, EARLY[0])

    for copy in sent_x:
        copy.wait_recv()
    by_x = []
    for kind in range(2):
        by_x.append(sum(table_x[kind, r : r + 1, :] * got_x[r] for r in range(nx)))
    g_x, h_x = by_x
    got_y[0] = jnp.where(row8 % 2 == 0, h_x + pltpu.roll(h_x, 7, 0), g_x + pltpu.roll(g_x, 1, 0))
    sent_y = [send(got_y.at[0], got_y.at[r], y_send.at[r], y_recv.at[r], (0, r, 0)) for r in range(1, ny)]

    for copy in faces:
        copy.wait_recv()
    for side, z in ((0, 0), (1, BZ - 1)):
        for c in range(COMPS):
            for n, (px, py) in enumerate(GHOST_COLUMNS):
                ghost_face[side, c, n : n + 1, :] = pad[px, py, c, z : z + 1, :]
    z_faces += [
        send(ghost_face.at[0], z_ghost.at[1], z_send.at[2], z_recv.at[2], (0, 0, -1)),
        send(ghost_face.at[1], z_ghost.at[0], z_send.at[3], z_recv.at[3], (0, 0, 1)),
    ]

    early_run(EARLY[0], EARLY[1])

    for copy in sent_y:
        copy.wait_recv()
    by_y = []
    for kind in range(2):
        pair = []
        for j in range(2):
            value = sum(table_y[kind, j, r] * got_y[r] for r in range(ny))
            pair.append(value + pltpu.roll(value, 4, 0))
        by_y.append(jnp.where(row8 < 4, pair[0], pair[1]))
    got_z[0] = exact_dot(by_y[0], fold_ref[0]) + exact_dot(by_y[1], fold_ref[1])
    sent_z = [send(got_z.at[0], got_z.at[r], far_send.at[r], far_recv.at[r], (0, 0, r)) for r in range(1, nz)]

    early_run(EARLY[0] + EARLY[1], EARLY[2])
    store((early, early_out))

    for copy in z_faces:
        copy.wait_recv()
    store((pad, pad_out), (z_own, z_own_out), (z_ghost, z_ghost_out))
    for px in range(PX):
        for py in range(PY):
            n = px * PY + py
            own_column = 1 <= px <= BX and 1 <= py <= BY
            if not own_column:
                code_rows[n, 1:5, :] = pad[px, py, 9]
            for side, at_row in ((0, 0), (1, 5)):
                if own_column:
                    i = (px - 1) * BY + py - 1
                    code_rows[n, at_row : at_row + 1, :] = z_own[side, 9, i : i + 1, :]
                else:
                    i = GHOST_COLUMNS.index((px, py))
                    code_rows[n, at_row : at_row + 1, :] = z_ghost[side, 9, i : i + 1, :]
    active = jnp.concatenate([active_inside, active_codes() * (1.0 - inside)], axis=0)
    gap = jnp.maximum(EARLY_ALL - early_total, 0.0)
    found, total = listed_tiles(active, jnp.concatenate([names, names], axis=0), LIST_ROWS, gap)
    for q, (owner, name) in enumerate(found):
        owner = jnp.where(owner < OWN, owner, owner - OWN)
        if q < 2:
            owner = jnp.where(iota((1, SEG), 1) + q * SEG < EARLY_ALL, early_found[q][0], owner)
        list_ref[q : q + 1, :] = owner.astype(jnp.int32)
        list_ref[8 + q : 9 + q, :] = name.astype(jnp.int32)
    list_ref[7:8, :] = total.astype(jnp.int32)
    list_ref[15:16, :] = jnp.zeros((1, SEG), jnp.int32)
    store((list_ref, list_out))

    for copy in sent_z:
        copy.wait_recv()
    field = []
    for k in range(2):
        value = sum(table_z[k, r] * got_z[r] for r in range(nz))
        field.append(value + pltpu.roll(value, 6, 0))
    far_ref[...] = exact_dot(jnp.concatenate(field, axis=0), fold_ref[2])
    store((far_ref, far_out))

    for copy in faces + z_faces + sent_x + sent_y + sent_z:
        copy.wait_send()
    for copy in stores:
        copy.wait()


def near_kernel(
    list_hbm, far_hbm, pad_hbm, z_own_hbm, z_ghost_hbm, source_hbm, weigh_hbm, target_hbm, place_hbm, early_hbm, node_hbm,
    force_out, velocity_out,
    list_ref, far_ref, pad, z_own, z_ghost, target, place_rows, early, node_ref,
    source, weigh, gathered, k_rows, q_rows, x_rows, in_sem,
):
    loads = []
    for i, (src, dst) in enumerate((
        (pad_hbm, pad), (z_own_hbm, z_own), (z_ghost_hbm, z_ghost), (source_hbm, source.at[0:OWN]),
        (weigh_hbm, weigh.at[0:OWN]), (target_hbm, target), (early_hbm, early), (list_hbm, list_ref),
        (far_hbm, far_ref), (place_hbm, place_rows), (node_hbm, node_ref),
    )):
        loads.append(pltpu.make_async_copy(src, dst, in_sem.at[i]))
        loads[-1].start()
    row8, lane8 = iota((8, SEG), 0), iota((8, SEG), 1)
    for ref in (gathered, k_rows, q_rows, x_rows):
        ref[...] = jnp.zeros_like(ref)
    for copy in loads[:3]:
        copy.wait()

    rows = (k_rows, q_rows, x_rows)
    step = 0
    for pair in range(len(GHOST_COLUMNS) // 2):
        columns = GHOST_COLUMNS[2 * pair : 2 * pair + 2]
        value = [jnp.concatenate([pad[px, py, c] for px, py in columns], axis=0) for c in range(9)]
        shifts = [[columns[i // 4][0] - 1.5 for i in range(8)], [columns[i // 4][1] - 2.5 for i in range(8)],
                  [i % 4 - 1.5 for i in range(8)]]
        features(step, COLUMN_GHOST + pair * 8, value, shifts, source, weigh, rows)
        step += 1
    for side in range(2):
        value = [z_own[side, c] for c in range(9)]
        shifts = [[n // 4 - 0.5 for n in range(8)], [n % 4 - 1.5 for n in range(8)], [side * 5 - 2.5] * 8]
        features(step, Z_OWN + side * 8, value, shifts, source, weigh, rows)
        step += 1
        for half in range(2):
            value = [z_ghost[side, c, half * 8 : half * 8 + 8, :] for c in range(9)]
            columns = GHOST_COLUMNS[half * 8 : half * 8 + 8]
            shifts = [[px - 1.5 for px, _ in columns], [py - 2.5 for _, py in columns], [side * 5 - 2.5] * 8]
            features(step, Z_GHOST + side * 16 + half * 8, value, shifts, source, weigh, rows)
            step += 1

    for copy in loads[3:]:
        copy.wait()
    per_row = SEG // CHUNK

    def add(t, value):
        gathered[pl.ds(pl.multiple_of(t * 8, 8), 8), :] += value

    def early_chunk(i, carry):
        list_row, start = i // per_row, lax.rem(i, per_row) * CHUNK
        for j in range(CHUNK):
            add(list_ref[list_row, start + j], early[i * CHUNK + j])
        return carry

    def chunk(i, carry):
        list_row, start = i // per_row, lax.rem(i, per_row) * CHUNK
        chosen = [(list_ref[list_row, start + j], list_ref[8 + list_row, start + j]) for j in range(CHUNK)]
        for (t, _), value in zip(chosen, near_tiles(chosen, target, source, weigh)):
            add(t, value)
        return carry

    lax.fori_loop(0, EARLY_ALL // CHUNK, early_chunk, 0)
    lax.fori_loop(EARLY_ALL // CHUNK, (list_ref[7, 0] + CHUNK - 1) // CHUNK, chunk, 0)

    for group in range(4):
        x, y = group // 2, group % 2 * 2

        def strided(r):
            return gathered[pl.ds(group * 64 + r, 8, stride=8), :]

        weights = strided(3)
        own = [jnp.concatenate([pad[x + 1, y + 1, c], pad[x + 1, y + 2, c]], axis=0) for c in range(3, 10)]
        burgers, line, count = own[0:3], own[3:6], own[6][:, 127:128]
        force = []
        for d in range(3):
            value = (strided(d) + strided(4 + d)) - place_rows[group, d] * weights
            x_row, kind = (0, 0) if d == 0 else (1, 1 if d == 1 else 0)
            for c in range(3):
                at = [far_ref[k * 8 + group % 2 * 4 + x_row, kind * 3 + c] for k in range(2)]
                value += jnp.where(row8 % 4 < 2, at[0], at[1]) * burgers[c]
            force.append(value)
            force_out[x, y, d] = value[0:4]
            force_out[x, y + 1, d] = value[4:8]
        nodes = [
            jnp.concatenate([node_ref[x, y, :, i, :], node_ref[x, y + 1, :, i, :]], axis=0) for i in range(2)
        ]

        def take(v, i):
            return jnp.take_along_axis(v, nodes[i], axis=1)

        node_force = [0.5 * (take(v, 0) + take(v, 1)) for v in force]
        b, t = [take(v, 0) for v in burgers], [take(v, 0) for v in line]
        normal = [t[1] * b[2] - t[2] * b[1], t[2] * b[0] - t[0] * b[2], t[0] * b[1] - t[1] * b[0]]
        along = node_force[0] * normal[0] + node_force[1] * normal[1] + node_force[2] * normal[2]
        size = jnp.maximum(normal[0] * normal[0] + normal[1] * normal[1] + normal[2] * normal[2], 1.0)
        ratio = (1.0 - CLIMB) * along / size
        live = lane8.astype(F32) < count
        for d in range(3):
            value = jnp.where(live, node_force[d] - ratio * normal[d], 0.0)
            velocity_out[x, y, d] = value[0:4]
            velocity_out[x, y + 1, d] = value[4:8]


def local(sizes, segments, seg_count, pair_offsets, pair_count, node_segs):
    nx, ny, nz = sizes
    by_component = jnp.transpose(segments, (0, 1, 3, 2, 4))
    table_x, table_y, table_z, fold = far_tables(nx, ny, nz)
    names = neighbour_table()
    vmem = pl.BlockSpec(memory_space=pltpu.VMEM)
    hbm = pl.BlockSpec(memory_space=pltpu.HBM)
    dma = pltpu.SemaphoreType.DMA
    operands = (
        by_component, seg_count, pair_offsets, pair_count,
        table_x, table_y, table_z, jnp.asarray(fold, BF16), names,
    )
    row_scratch = [pltpu.VMEM((2, 9 * 32, SEG), F32)] * 2 + [pltpu.VMEM((2, 9 * 16, SEG), F32)]
    results = (
        jax.ShapeDtypeStruct((PX, PY, COMPS, BZ, SEG), F32),
        jax.ShapeDtypeStruct((2, COMPS, 8, SEG), F32),
        jax.ShapeDtypeStruct((2, COMPS, 16, SEG), F32),
        jax.ShapeDtypeStruct((16, SEG), jnp.int32),
        jax.ShapeDtypeStruct((16, SEG), F32),
        jax.ShapeDtypeStruct((OWN, 64, 2 * SEG), BF16),
        jax.ShapeDtypeStruct((OWN, 16, 2 * SEG), BF16),
        jax.ShapeDtypeStruct((OWN + 1, SEG, 64), BF16),
        jax.ShapeDtypeStruct((4, 3, 8, SEG), F32),
        jax.ShapeDtypeStruct((EARLY_ALL, 8, SEG), F32),
    )
    held = [pltpu.VMEM(v.shape, v.dtype) for v in results]
    made = pl.pallas_call(
        functools.partial(exchange_kernel, sizes),
        out_shape=results,
        in_specs=[hbm] * 9,
        out_specs=(hbm,) * 10,
        scratch_shapes=held + [pltpu.VMEM(v.shape, v.dtype) for v in operands] + [
            pltpu.VMEM((2, COMPS, 8, SEG), F32),
            pltpu.VMEM((2, COMPS, 16, SEG), F32),
            pltpu.VMEM((nx, 8, SEG), F32),
            pltpu.VMEM((ny, 8, SEG), F32),
            pltpu.VMEM((nz, 8, SEG), F32),
            pltpu.VMEM((PX * PY, 8, SEG), F32),
        ] + row_scratch + [
            pltpu.VMEM((2, 9 * 64, SEG), F32),
            pltpu.VMEM((8, SEG), jnp.int32),
            pltpu.SMEM((8, SEG), jnp.int32),
            dma((9,)), dma((10,)), dma,
            dma((8,)), dma((8,)), dma((4,)), dma((4,)),
            dma((nx,)), dma((nx,)), dma((ny,)), dma((ny,)), dma((nz,)), dma((nz,)),
        ],
        compiler_params=pltpu.CompilerParams(collective_id=0, has_side_effects=True, vmem_limit_bytes=VMEM_LIMIT),
        name="exchange",
    )(*operands)
    pad, z_own, z_ghost, tiles, far, source, weigh, target, place, early = made
    force, velocity = pl.pallas_call(
        near_kernel,
        out_shape=(jax.ShapeDtypeStruct((BX, BY, 3, BZ, SEG), F32),) * 2,
        in_specs=[hbm] * 11,
        out_specs=(vmem, vmem),
        scratch_shapes=[
            pltpu.SMEM((16, SEG), jnp.int32),
            pltpu.SMEM((16, SEG), F32),
            held[0], held[1], held[2], held[7], held[8], held[9],
            pltpu.VMEM(node_segs.shape, node_segs.dtype),
            pltpu.VMEM((BLOCKS, 64, 2 * SEG), BF16),
            pltpu.VMEM((BLOCKS, 16, 2 * SEG), BF16),
            pltpu.VMEM(((OWN + 1) * 8, SEG), F32),
        ] + row_scratch + [dma((11,))],
        compiler_params=pltpu.CompilerParams(vmem_limit_bytes=VMEM_LIMIT),
        name="near",
    )(tiles, far, pad, z_own, z_ghost, source, weigh, target, place, early, node_segs)
    return tuple(jnp.transpose(v, (0, 1, 3, 2, 4)) for v in (force, velocity))


def solution(mesh):
    sizes = tuple(mesh.shape[axis] for axis in ("gx", "gy", "gz"))
    placed = (
        P("gx", "gy", "gz", None, None),
        P("gx", "gy", "gz"),
        P("gx", "gy", "gz", None),
        P("gx", "gy", "gz"),
        P("gx", "gy", "gz", None, None),
    )
    return jax.shard_map(
        functools.partial(local, sizes),
        mesh=mesh,
        in_specs=placed,
        out_specs=(P("gx", "gy", "gz", None, None), P("gx", "gy", "gz", None, None)),
        check_vma=False,
    )
```

time: 63.3 us -> 44.4 us (0.70)
  the two profiles are of different devices: /device:TPU:24 before, /device:TPU:1 now
where the time goes in v2:
time: 44.4 us; the launch traced here: 44.3 us
  Pallas kernels  43.7 us (98%)
  between operations  0.64 us (1%)
    pallas_call x1, Pallas kernels, local(): pl.pallas_call(functools.partial(exchange_kernel, sizes), out_shape=resul...  33 us
    pallas_call x1, Pallas kernels, local(): pl.pallas_call(near_kernel, out_shape=(jax.ShapeDtypeStruct((BX, BY, 3, B...  10.6 us

profile of v2, /device:TPU:1, one launch (start us, length us, event | category | flops | bytes accessed | tf_op | source)
XLA Modules:
  0.0 44.3 jit_solution(10936146264245932598)
XLA Ops:
  0.6 33.0 %exchange.1 = (f32[4,6,10,4,128]{4,3,2,1,0:T(4,128)}, f32[2,10,8,128]{3,2,1,0:T(8,128)}, f32[2,10,16,128]{3,2,1,0:T(8,128)}, s32[16,128]{1,0:T(8,128)}, f32[16,1...) custom-call(f32[2,4,9,4,128]{4,3,2,1,0:T(4,128)} %bitcast.3, ...), custom_call_target="tpu_custom_call" | custom-call | tf_op jit(solution)/shard_map/exchange/pallas_call | solution.py:671
  33.7 10.6 %near.1 = (f32[2,4,3,4,128]{4,3,2,1,0:T(4,128)}, f32[2,4,3,4,128]{4,3,2,1,0:T(4,128)}) custom-call(s32[16,128]{1,0:T(8,128)} %get-tuple-element.14.list_hbm, f32[16,128]{1,0:T(8,128)} %get-tuple-element.15.far_hbm, f32[4,6,10,4,128]{4,3,2,1,0:T(4,128)} %get-tuple-element.16.pad_hbm, f32[2,10,8,128]{3,2,1,0:T(8,128)} %get-tuple-element.17.z_own_hbm, ...), custom_call_target="tpu_custom_call" | custom-call | tf_op jit(solution)/shard_map/near/pallas_call | solution.py:695
